TPU v7x, 128 devices: a whole 4x4x4 slice. The times are simulated.
128 devices in a mesh: pb: 16 (over y, z), ta: 8 (over x, core).
Axes of the slice: x: 4, y: 4, z: 4, core: 2. Of those that a mesh axis runs over, the one named last changes fastest.
Arguments:
- coeffs: bfloat16 [128, 128, 16384], P('pb', None, 'ta'), may hold values from -6 to 6
- elph_table: bfloat16 [9, 16384], replicated, may hold values from -0.046875 to 0.046875
- energies: float32 [128, 128], replicated, may hold values from 1.6 to 1.7
- phonon_energy: float32 [9], replicated, may hold values from 0.005 to 0.035
- deviation: float32 [128, 128], replicated, may hold values from 0.2 to 2
- source: float32 [128, 128], P('pb'), may hold values from -6 to 6
- inv_tau: float32 [128, 128], P('pb'), may hold values from 0.5 to 5
- block_pairs: int32 [192, 2], replicated, may hold values from 0 to 127, as said below
- mode_index: int32 [192, 9], replicated, may hold values from 0 to 8, each once within a row
- offsets: int32 [192], replicated, may hold values from 0 to 16383
Outputs:
- new_deviation: float32 [128, 128], P('pb')
- linewidth: float32 [128, 128], P('pb')
Inputs may be any that keep to these rules, and one draw needn't show every extreme that they name: `block_pairs`: block n lies on device n // 8 of pb. Exactly 12 pairs have their second block on each device; at most 24 pairs have their first block on one device, and one device has exactly 24. For one device of first blocks and one device of second blocks there are at most 2 pairs, and some such couple of devices has exactly 2 in every draw. `mode_index`: each row names every branch once.
All inputs are finite; a program needn't handle non-finite values.
Results may differ from a plain program's by a relative error of at most 0.0003.
Values may be sent and summed in bfloat16 or wider, within the bound.
A program may use at most 128 MiB of HBM per device.

v0:
```python
import jax
import jax.numpy as jnp
from jax import lax
from jax.sharding import PartitionSpec as P

PAIRS_DEV = 12


BOLTZMANN_KT = 0.02585
BROADENING = 0.01


def pair_rates(coupling, energy_first, energy_second, phonon_energy):
    bose_factor = 1.0 / (jnp.exp(phonon_energy / BOLTZMANN_KT) - 1.0)
    detuning = energy_first[:, None] - energy_second[None, :]
    omega_mode = phonon_energy[:, None, None]
    lorentz_minus = 1.0 / (1.0 + ((detuning[None] - omega_mode) / BROADENING) ** 2)
    lorentz_plus = 1.0 / (1.0 + ((detuning[None] + omega_mode) / BROADENING) ** 2)
    strength = coupling * coupling / (coupling.shape[0] * coupling.shape[2])
    occupation = bose_factor[:, None, None]
    forward = strength * ((occupation + 1.0) * lorentz_minus + occupation * lorentz_plus)
    backward = strength * ((occupation + 1.0) * lorentz_plus + occupation * lorentz_minus)
    return (forward, backward)


def pair_flows(forward, backward, value_first, value_second):
    out_first = jnp.sum(forward, axis=(0, 2))
    in_first = jnp.sum(backward * value_second[None, None, :], axis=(0, 2))
    out_second = jnp.sum(backward, axis=(0, 1))
    in_second = jnp.sum(forward * value_first[None, :, None], axis=(0, 1))
    return (out_first, in_first, out_second, in_second)


def shards(
    coeffs,
    elph_table,
    energies,
    phonon_energy,
    deviation,
    source,
    inv_tau,
    block_pairs,
    mode_index,
    offsets,
):
    block_count, state_rows, trans_local = coeffs.shape
    mode_count = elph_table.shape[0]
    pb_count = lax.axis_size("pb")
    my_device = lax.axis_index("pb")
    ta_place = lax.axis_index("ta")
    busiest = 2 * PAIRS_DEV
    capacity = max(2, (busiest + pb_count - 1) // pb_count)
    slot_count = pb_count * capacity
    pair_total = block_pairs.shape[0]
    owners = block_pairs // block_count
    places = block_pairs % block_count
    cell_index = owners[:, 0] * pb_count + owners[:, 1]
    row_iota = lax.broadcasted_iota(jnp.int32, (pair_total, pair_total), 0)
    col_iota = lax.broadcasted_iota(jnp.int32, (pair_total, pair_total), 1)
    earlier_same = (cell_index[:, None] == cell_index[None, :]) & (col_iota < row_iota)
    pair_rank = jnp.sum(earlier_same.astype(jnp.int32), axis=1)
    near_column = 0
    near_owner = owners[:, near_column]
    far_owner = owners[:, 1 - near_column]
    near_place = places[:, near_column]
    far_place = places[:, 1 - near_column]
    send_slot = near_owner * capacity + pair_rank
    slot_iota = lax.broadcasted_iota(jnp.int32, (slot_count, pair_total), 0)
    outgoing = (far_owner[None, :] == my_device) & (send_slot[None, :] == slot_iota)
    send_place = jnp.sum(jnp.where(outgoing, far_place[None, :], 0), axis=1)
    send_live = jnp.any(outgoing, axis=1)
    send_blocks = jnp.take(coeffs, send_place, axis=0).reshape(
        pb_count, capacity, state_rows, trans_local
    )
    far_blocks = lax.all_to_all(send_blocks, "pb", split_axis=0, concat_axis=0, tiled=True)
    far_flat = far_blocks.reshape(slot_count, state_rows, trans_local)
    is_mine = near_owner == my_device
    position = jnp.cumsum(is_mine.astype(jnp.int32)) - 1
    list_iota = lax.broadcasted_iota(jnp.int32, (busiest, pair_total), 0)
    chosen = is_mine[None, :] & (position[None, :] == list_iota)

    def pick_values(values):
        return jnp.sum(jnp.where(chosen, values[None, :], 0), axis=1)

    item_live = jnp.any(chosen, axis=1)
    recv_slot = pick_values(far_owner * capacity + pair_rank)
    near_pick = pick_values(near_place)
    first_pick = pick_values(block_pairs[:, 0])
    second_pick = pick_values(block_pairs[:, 1])
    item_offset = pick_values(offsets)
    item_modes = jnp.sum(jnp.where(chosen[:, :, None], mode_index[None, :, :], 0), axis=1)
    doubled = jnp.concatenate([elph_table, elph_table], axis=1)
    start_base = ta_place * trans_local
    item_arrays = (recv_slot, near_pick, item_offset, item_modes)

    def couple(pair_item, row_count):
        slot_index, near_index, offset_one, mode_rows = pair_item
        far_block = lax.dynamic_index_in_dim(far_flat, slot_index, 0, keepdims=False)
        near_block = lax.dynamic_index_in_dim(coeffs, near_index, 0, keepdims=False)
        coeff_first, coeff_second = (near_block, far_block)
        window = lax.dynamic_slice_in_dim(doubled, offset_one + start_base, trans_local, 1)
        coupling_table = jnp.take(window, mode_rows, axis=0)
        scaled = (
            coeff_first[None].astype(jnp.float32) * coupling_table[:, None, :].astype(jnp.float32)
        ).astype(jnp.bfloat16)
        product = lax.dot_general(
            scaled.reshape(mode_count * row_count, trans_local),
            coeff_second,
            (((1,), (1,)), ((), ())),
            preferred_element_type=jnp.float32,
        )
        return product.reshape(mode_count, row_count, state_rows)

    partials = lax.map(lambda pair_item: couple(pair_item, state_rows), item_arrays)
    coupling = lax.psum(partials, "ta")
    energy_first = jnp.take(energies, first_pick, axis=0)
    value_first = jnp.take(deviation, first_pick, axis=0)
    energy_second = jnp.take(energies, second_pick, axis=0)
    value_second = jnp.take(deviation, second_pick, axis=0)

    def flow_terms(pair_item):
        coupling_one, energy_one, energy_two, value_one, value_two = pair_item
        forward, backward = pair_rates(coupling_one, energy_one, energy_two, phonon_energy)
        return pair_flows(forward, backward, value_one, value_two)

    out_first, in_first, out_second, in_second = lax.map(
        flow_terms, (coupling, energy_first, energy_second, value_first, value_second)
    )
    live_scale = item_live.astype(jnp.float32)[:, None, None]
    first_terms = jnp.stack([out_first, in_first], axis=1) * live_scale
    second_terms = jnp.stack([out_second, in_second], axis=1) * live_scale
    near_terms, far_terms = (first_terms, second_terms)
    block_iota = lax.broadcasted_iota(jnp.int32, (block_count, busiest), 0)
    near_hot = (near_pick[None, :] == block_iota).astype(jnp.float32)
    totals = jnp.einsum("bk,kcr->bcr", near_hot, near_terms, precision=lax.Precision.HIGHEST)
    back_iota = lax.broadcasted_iota(jnp.int32, (slot_count, busiest), 0)
    back_hot = (recv_slot[None, :] == back_iota).astype(jnp.float32)
    back_send = jnp.einsum(
        "sk,kcr->scr", back_hot, far_terms, precision=lax.Precision.HIGHEST
    ).reshape(pb_count, capacity, 2, state_rows)
    back_recv = lax.all_to_all(back_send, "pb", split_axis=0, concat_axis=0, tiled=True).reshape(
        slot_count, 2, state_rows
    )
    send_iota = lax.broadcasted_iota(jnp.int32, (block_count, slot_count), 0)
    send_hot = ((send_place[None, :] == send_iota) & send_live[None, :]).astype(jnp.float32)
    totals = totals + jnp.einsum(
        "bs,scr->bcr", send_hot, back_recv, precision=lax.Precision.HIGHEST
    )
    outflow = totals[:, 0]
    inflow = totals[:, 1]
    return ((source + inflow) / (inv_tau + outflow), outflow)


def solution(mesh):
    in_specs = (
        P("pb", None, "ta"),
        P(),
        P(),
        P(),
        P(),
        P("pb", None),
        P("pb", None),
        P(),
        P(),
        P(),
    )
    out_specs = (P("pb", None), P("pb", None))
    return jax.shard_map(shards, mesh=mesh, in_specs=in_specs, out_specs=out_specs, check_vma=False)
```

profile of v0, /device:TPU:1, one launch (start us, length us, event | category | flops | bytes accessed | tf_op | source)
XLA Modules:
  0.0 835.5 jit_solution(12883881295773925608)
XLA Ops:
  8.4 9.3 %gather_fusion.1 = bf16[32,128,2048]{2,1,0:T(8,128)(2,1)} fusion(bf16[8,128,2048]{2,1,0:T(8,128)(2,1)} %param.16, s32[1024]{0:T(1024)S(1)} %pad_clamp_fusion.3), kind=kCustom, calls=%fused_computation.5 | custom fusion | bytes 33554560 | tf_op jit(solution)/shard_map/jit(_take)/gather | solution.py:72
  17.7 14.2 %broadcast_select_fusion = bf16[16,2,128,2048]{3,2,1,0:T(8,128)(2,1)} fusion(bf16[16,2,128,2048]{3,2,1,0:T(8,128)(2,1)} %bitcast.109, pred[16,2]{1,0:T(8,128)(4,1)S(1)} %compare_and_fusion.1), kind=kLoop, calls=%fused_computation.42 | loop fusion | flops 8388608 | bytes 33554464 | tf_op jit(solution)/shard_map/jit(_take)/select_n | solution.py:72
  31.9 8.8 %all-to-all-start = ((bf16[16,2,128,2048]{3,2,1,0:T(8,128)(2,1)}), bf16[16,2,128,2048]{3,2,1,0:T(8,128)(2,1)}, u32[]{:S(2)}, u32[]{:S(2)}) async-start(bf16[16,2,128,2048]{3,2,1,0:T(8,128)(2,1)} %broadcast_select_fusion), calls=%async_computation | async-start | bytes 33554432 | tf_op jit(solution)/shard_map/all_to_all | solution.py:75
  42.1 291.0 %all-to-all-done = bf16[16,2,128,2048]{3,2,1,0:T(8,128)(2,1)} async-done(((bf16[16,2,128,2048]{3,2,1,0:T(8,128)(2,1)}), bf16[16,2,128,2048]{3,2,1,0:T(8,128)(2,1)}, u32[]{:S(2)}, u32[]{:S(2)}) %all-to-all-start) | async-done | bytes 16777248 | tf_op jit(solution)/shard_map/all_to_all | solution.py:75
  333.2 262.6 %while.28 = (s32[]{:T(128)}, f32[24,9,128,128]{3,2,1,0:T(8,128)}, s32[24]{0:T(128)S(1)}, bf16[8,128,2048]{2,1,0:T(8,128)(2,1)}, s32[24,9]{1,0:T(8,128)S(1)}, /*i...) while((s32[]{:T(128)}, f32[24,9,128,128]{3,2,1,0:T(8,128)}, ...), condition=%wide.region_9.10_spmd, body=%wide.region_8.9_spmd.sunk | while | flops 608998464 | bytes 4072445 | solution.py:114
  340.8 3.3 fusion.56
  351.8 3.3 fusion.56
  362.7 3.3 fusion.56
  373.7 3.2 fusion.56
  384.6 3.3 fusion.56
  395.6 3.3 fusion.56
  406.5 3.3 fusion.56
  417.5 3.3 fusion.56
  428.4 3.3 fusion.56
  439.3 3.3 fusion.56
  450.3 3.2 fusion.56
  461.2 3.3 fusion.56
  472.2 3.2 fusion.56
  483.1 3.3 fusion.56
  494.0 3.3 fusion.56
  505.0 3.3 fusion.56
  515.9 3.3 fusion.56
  526.9 3.3 fusion.56
  537.8 3.3 fusion.56
  548.8 3.3 fusion.56
  559.7 3.3 fusion.56
  570.6 3.3 fusion.56
  581.6 3.3 fusion.56
  592.5 3.3 fusion.56
  598.7 161.8 %all-reduce.3.cloned.1.call-done = f32[24,9,128,128]{3,2,1,0:T(8,128)} async-done(((f32[24,9,128,128]{3,2,1,0:T(8,128)}), f32[24,9,128,128]{3,2,1,0:T(8,128)}) %all-reduce.3.cloned.1.call-update) | async-done | bytes 14155792 | tf_op jit(solution)/shard_map/psum | solution.py:115
  760.5 53.3 %while.29 = (s32[]{:T(128)}, f32[24,128]{1,0:T(8,128)S(1)}, f32[24,128]{1,0:T(8,128)S(1)}, f32[24,128]{1,0:T(8,128)S(1)}, f32[24,128]{1,0:T(8,128)S(1)}, /*index...) while((s32[]{:T(128)}, f32[24,128]{1,0:T(8,128)S(1)}, ...), condition=%wide.region_18.20_spmd, body=%wide.region_13.19_spmd.sunk | while | flops 3849766 | bytes 3092849 | solution.py:126
  760.6 1.5 bitcast_multiply_fusion.3
  767.3 1.5 bitcast_multiply_fusion.3
  769.5 1.5 bitcast_multiply_fusion.3
  771.7 1.5 bitcast_multiply_fusion.3
  778.4 1.5 bitcast_multiply_fusion.3
  780.6 1.5 bitcast_multiply_fusion.3
  782.8 1.5 bitcast_multiply_fusion.3
  787.3 1.5 bitcast_multiply_fusion.3
  789.5 1.5 bitcast_multiply_fusion.3
  791.7 1.5 bitcast_multiply_fusion.3
  798.4 1.5 bitcast_multiply_fusion.3
  800.6 1.5 bitcast_multiply_fusion.3
  802.8 1.5 bitcast_multiply_fusion.3
  809.5 1.5 bitcast_multiply_fusion.3
  811.7 1.5 bitcast_multiply_fusion.3
  814.7 6.7 all-to-all-start.1
  821.6 6.3 all-to-all-done.1
  (557 shorter events, 124.7 us)
Async XLA Ops:
  7.2 588.7 %copy-start = (f32[128,128]{1,0:T(8,128)S(1)}, f32[128,128]{1,0:T(8,128)}, u32[]{:S(2)}) copy-start(f32[128,128]{1,0:T(8,128)} %param.18) | copy-start | bytes 196612
  31.9 9.6 %copy-start.3 = (s32[192,9]{0,1:T(8,128)S(1)}, s32[192,9]{0,1:T(8,128)}, u32[]{:S(2)}) copy-start(s32[192,9]{0,1:T(8,128)} %param.24) | copy-start | bytes 20740
  31.9 9.9 %copy-start.5 = (s32[192,2]{0,1:T(2,128)S(1)}, s32[192,2]{0,1:T(2,128)}, u32[]{:S(2)}) copy-start(s32[192,2]{0,1:T(2,128)} %param.23) | copy-start | bytes 4612
  31.9 9.9 %copy-start.8 = (s32[192]{0:T(256)S(1)}, s32[192]{0:T(256)}, u32[]{:S(2)}) copy-start(s32[192]{0:T(256)} %param.25) | copy-start | bytes 2308
  31.9 10.1 %copy-start.2 = (bf16[9,16384]{1,0:T(8,128)(2,1)S(1)}, bf16[9,16384]{1,0:T(8,128)(2,1)}, u32[]{:S(2)}) copy-start(bf16[9,16384]{1,0:T(8,128)(2,1)} %param.17) | copy-start | bytes 884740
  31.9 301.3 %all-to-all-start = ((bf16[16,2,128,2048]{3,2,1,0:T(8,128)(2,1)}), bf16[16,2,128,2048]{3,2,1,0:T(8,128)(2,1)}, u32[]{:S(2)}, u32[]{:S(2)}) async-start(bf16[16,2,128,2048]{3,2,1,0:T(8,128)(2,1)} %broadcast_select_fusion), calls=%async_computation | async-start | bytes 33554432 | tf_op jit(solution)/shard_map/all_to_all | solution.py:75
  40.6 719.8 %all-reduce.3.cloned.1.call-start = ((), (), s32[]{:S(2)}) async-start(), calls=%async_computation.2 | async-start | bytes 28311552 | tf_op jit(solution)/shard_map/psum | solution.py:115
  595.8 0.8 copy-start.1
  595.8 164.7 %copy-start.4 = (f32[9]{0:T(128)S(1)}, f32[9]{0:T(128)}, u32[]{:S(2)}) copy-start(f32[9]{0:T(128)} %param.19) | copy-start | bytes 112
  595.8 232.3 %copy-start.6 = (f32[8,128]{1,0:T(8,128)S(1)}, f32[8,128]{1,0:T(8,128)}, u32[]{:S(2)}) copy-start(f32[8,128]{1,0:T(8,128)} %param.21) | copy-start | bytes 12292
  595.8 232.3 %copy-start.7 = (f32[8,128]{1,0:T(8,128)S(1)}, f32[8,128]{1,0:T(8,128)}, u32[]{:S(2)}) copy-start(f32[8,128]{1,0:T(8,128)} %param.22) | copy-start | bytes 12292
  814.7 13.2 %all-to-all-start.1 = ((f32[16,2,2,128]{3,1,2,0:T(2,128)}), f32[16,2,2,128]{3,1,2,0:T(2,128)S(1)}, u32[]{:S(2)}, u32[]{:S(2)}) async-start(f32[16,2,2,128]{3,1,2,0:T(2,128)} %copy.18), calls=%async_computation.1 | async-start | bytes 65536 | tf_op jit(solution)/shard_map/all_to_all | solution.py:141
Sparse Core Ops, SparseCore 0:
  595.9 164.4 all-reduce.2
where the time goes:
time: 842 us; the launch traced here: 836 us
  waiting for transfers between devices  459 us (55%)
  loops' own time  97.1 us (12%)
  other arithmetic  95.8 us (11%)
  matrix products  79.1 us (9%)
  local copies, waits for them, and re-layouts  74.6 us (9%)
  starting transfers between devices  15.5 us (2%)
  between operations  14.3 us (2%)
    all_to_all x1, waiting for transfers between devices, shards(): lax.all_to_all(send_blocks, 'pb', split_axis=0, concat_axis=0, tiled=True)  291 us
    psum x1, waiting for transfers between devices, shards(): coupling = lax.psum(partials, 'ta')  162 us
    another operation x1, loops' own time, shards(): lax.map(lambda pair_item: couple(pair_item, state_rows), item_arrays)  95.9 us
    dot_general x24, matrix products, couple(): lax.dot_general(scaled.reshape(mode_count * row_count, trans_local), coef...  78.5 us
    dynamic_slice x72, local copies, waits for them, and re-layouts, shards(): lax.map(lambda pair_item: couple(pair_item, state_rows), item_arrays)  41.9 us
    mul x24, other arithmetic, pair_rates(): strength * ((occupation + 1.0) * lorentz_plus + occupation * lorentz_minus)  36.5 us
    mul x24, other arithmetic, couple(): coeff_first[None].astype(jnp.float32)  27.3 us
  transfers between devices with their start and end apart: 3, of which 3 were waited for; matrix products, arithmetic and copies ran while one was open for 0% of the time, Pallas kernels for 0%

commit v1 on v0

v1 whole, which is shorter than its diff:
```python
import jax
import jax.numpy as jnp
from jax import lax
from jax.experimental import pallas as pl
from jax.experimental.pallas import tpu as pltpu
from jax.sharding import PartitionSpec as P

PAIRS_DEV = 12
BOLTZMANN_KT = 0.02585
BROADENING = 0.01
MESH = pl.DeviceIdType.MESH
LANES = 128
INTS = 5

MOVES = (
    (1, 0), (0, 1), (3, 0), (0, 3), (1, 1), (3, 3), (1, 3), (3, 1),
    (2, 0), (0, 2), (2, 1), (1, 2), (2, 3), (3, 2), (2, 2),
)


def pair_lists(block_pairs, mode_index, offsets, phonon_energy, block_count, low, trans_all):
    pair_total, mode_count = mode_index.shape
    start = lax.rem(offsets + low, trans_all)
    columns = (
        block_pairs[:, 0], block_pairs[:, 1], lax.rem(block_pairs[:, 1], block_count),
        lax.div(start, LANES), lax.rem(start, LANES),
    )
    owner = block_pairs[:, 1] // block_count
    serial = jnp.arange(pair_total, dtype=jnp.int32)
    earlier = (owner[:, None] == owner[None, :]) & (serial[None, :] < serial[:, None])
    slot = owner * PAIRS_DEV + jnp.sum(earlier.astype(jnp.int32), axis=1)
    hot = slot[None, :] == serial[:, None]
    data = jnp.concatenate([jnp.stack(columns, axis=1), mode_index], axis=1)
    data = jnp.sum(jnp.where(hot[:, :, None], data[None], 0), axis=1)
    modes = data[:, INTS:]
    rows = jnp.arange(mode_count, dtype=jnp.int32)
    at_row = modes[:, None, :] == rows[None, :, None]
    energy = jnp.sum(jnp.where(at_row, phonon_energy[None, None, :], 0.0), axis=2)
    bose = 1.0 / (jnp.exp(energy / BOLTZMANN_KT) - 1.0)
    values = jnp.concatenate([energy, bose], axis=1)
    return data[:, :INTS].reshape(-1), values.reshape(-1)


def kernel(
    ints, values, coeffs, table, energies, deviation, source, inv_tau,
    new_out, line_out,
    pieces, stage, other, part_out, part_in, weight_f, weight_b, value_a, wide, window,
    turn, acc_first, acc_second, first_in, second_in, total, total_in,
    send1, recv1, send2, recv2, send3, recv3, send4, recv4,
):
    blocks, rows, trans = coeffs.shape
    modes, trans_all = table.shape
    pair_count = other.shape[0]
    my_pb = lax.axis_index("pb")
    my_ta = lax.axis_index("ta")
    pb_count = 16
    ta_count = 8
    width = trans // pb_count
    strip = rows // ta_count
    my_y, my_z = my_pb // 4, my_pb % 4
    peers = [((my_y + dy) % 4) * 4 + (my_z + dz) % 4 for dy, dz in MOVES]
    mates = [(my_ta + d) % ta_count for d in range(1, ta_count)]
    n_peers, n_mates = len(peers), len(mates)

    barrier = pltpu.get_barrier_semaphore()
    for peer in peers:
        pl.semaphore_signal(barrier, inc=1, device_id=(peer, my_ta), device_id_type=MESH)
    for mate in mates:
        pl.semaphore_signal(barrier, inc=1, device_id=(my_pb, mate), device_id_type=MESH)
    pl.semaphore_wait(barrier, n_peers + n_mates)

    def remote(src, dst, send, recv, device):
        return pltpu.make_async_remote_copy(
            src_ref=src, dst_ref=dst, send_sem=send, recv_sem=recv,
            device_id=device, device_id_type=MESH,
        )

    my_lane = pl.multiple_of(my_pb * width, width)

    def spread(c, carry):
        for k, peer in enumerate(peers):
            lane = pl.multiple_of(peer * width, width)
            remote(
                coeffs.at[c, :, pl.ds(lane, width)], pieces.at[my_pb * blocks + c],
                send1.at[k], recv1.at[k], (peer, my_ta),
            ).start()
        pieces[my_pb * blocks + c] = coeffs[c, :, pl.ds(my_lane, width)]
        return carry

    lax.fori_loop(0, blocks, spread, 0)

    wide[...] = jnp.zeros_like(wide)
    tiles_all = trans_all // LANES

    def widen(tile, carry):
        lane = pl.multiple_of(lax.rem(tile, tiles_all) * LANES, LANES)
        wide[tile, pl.ds(0, modes), :] = table[:, pl.ds(lane, LANES)].astype(jnp.float32)
        return carry

    lax.fori_loop(0, wide.shape[0], widen, 0)
    acc_first[...] = jnp.zeros_like(acc_first)
    acc_second[...] = jnp.zeros_like(acc_second)

    def number(s, which):
        return ints[(my_pb * pair_count + s) * INTS + which]

    def strip_of(source_ref, block):
        row = source_ref[pl.ds(block, 1), :]
        turn[0] = jnp.transpose(jnp.broadcast_to(row, (rows, rows)))
        return turn[0, pl.ds(pl.multiple_of(my_ta * strip, strip), strip), :]

    def prepare(s, carry):
        first, second, tile, shift = number(s, 0), number(s, 1), number(s, 3), number(s, 4)
        tiles = trans // LANES
        piece = wide[pl.ds(tile, tiles + 1)]
        amount = jnp.full(piece.shape, shift, jnp.int32)
        for bit in range(7):
            moved = pltpu.roll(piece, LANES - (1 << bit), 2)
            piece = jnp.where((amount & (1 << bit)) != 0, moved, piece)
        lane = lax.broadcasted_iota(jnp.int32, (16, LANES), 1)
        keep = lane < LANES - amount[0]
        for t in range(tiles):
            window[s, :, t * LANES:(t + 1) * LANES] = jnp.where(keep, piece[t], piece[t + 1])
        detuning = strip_of(energies, first) - energies[pl.ds(second, 1), :]
        base = (my_pb * pair_count + s) * (2 * modes)
        for r in range(modes):
            energy = values[base + r]
            bose = values[base + modes + r]
            minus = 1.0 / (1.0 + ((detuning - energy) / BROADENING) ** 2)
            plus = 1.0 / (1.0 + ((detuning + energy) / BROADENING) ** 2)
            scale = 1.0 / (modes * rows)
            weight_f[s, r] = ((bose + 1.0) * minus + bose * plus) * scale
            weight_b[s, r] = ((bose + 1.0) * plus + bose * minus) * scale
        value_a[s] = strip_of(deviation, first)
        return carry

    lax.fori_loop(0, pair_count, prepare, 0)

    for k, peer in enumerate(peers):
        lane = pl.multiple_of(peer * width, width)
        copy = remote(
            coeffs.at[:, :, pl.ds(lane, width)], pieces.at[pl.ds(my_pb * blocks, blocks)],
            send1.at[k], recv1.at[k], (peer, my_ta),
        )
        copy.wait_send()
        copy.wait_recv()

    def deliver(s, carry):
        for k, peer in enumerate(peers):
            stage[s, k] = pieces[ints[(peer * pair_count + s) * INTS]]
            remote(
                stage.at[s, k], other.at[s, :, pl.ds(my_lane, width)],
                send2.at[s], recv2.at[s], (peer, my_ta),
            ).start()
        other[s, :, pl.ds(my_lane, width)] = pieces[number(s, 0)]
        return carry

    lax.fori_loop(0, pair_count, deliver, 0)

    def flows(s):
        copy = remote(
            part_in.at[s, pl.ds(0, n_mates)], part_in.at[s, pl.ds(0, n_mates)],
            send3.at[s], recv3.at[s], (my_pb, mates[0]),
        )
        copy.wait_send()
        copy.wait_recv()
        coupling = part_in[s, 0].astype(jnp.float32)
        for q in range(1, ta_count):
            coupling = coupling + part_in[s, q].astype(jnp.float32)
        square = coupling * coupling
        forward = jnp.sum(square * weight_f[s], axis=0)
        backward = jnp.sum(square * weight_b[s], axis=0)
        first, second = number(s, 0), number(s, 1)
        value_b = deviation[pl.ds(second, 1), :]
        out_first = jnp.sum(forward, axis=1, keepdims=True)
        in_first = jnp.sum(backward * value_b, axis=1, keepdims=True)
        out_second = jnp.sum(backward, axis=0, keepdims=True)
        in_second = jnp.sum(forward * value_a[s], axis=0, keepdims=True)
        here = lax.broadcasted_iota(jnp.int32, (strip, rows), 1) == first
        acc_first[0] += jnp.where(here, out_first, 0.0)
        acc_first[1] += jnp.where(here, in_first, 0.0)
        there = lax.broadcasted_iota(jnp.int32, (blocks, rows), 0) == number(s, 2)
        acc_second[0] += jnp.where(there, out_second, 0.0)
        acc_second[1] += jnp.where(there, in_second, 0.0)

    def couple(s, carry):
        copy = remote(
            stage.at[s], stage.at[s], send2.at[s], recv2.at[s], (peers[0], my_ta),
        )
        copy.wait_send()
        copy.wait_recv()
        place = number(s, 2)

        def one_mode(r, inner):
            row = window[s, pl.ds(r, 1), :]
            scale = jnp.broadcast_to(row, (16, trans)).astype(jnp.bfloat16)
            scaled = other[s].reshape(rows // 16, 16, trans) * scale[None]
            product = lax.dot_general(
                scaled.reshape(rows, trans), coeffs[place],
                (((1,), (1,)), ((), ())), preferred_element_type=jnp.float32,
            )
            part_out[s, r] = product.astype(jnp.bfloat16)
            return inner

        lax.fori_loop(0, modes, one_mode, 0)
        for mate in mates:
            remote(
                part_out.at[s, :, pl.ds(pl.multiple_of(mate * strip, strip), strip), :],
                part_in.at[s, my_ta], send3.at[s], recv3.at[s], (my_pb, mate),
            ).start()
        part_in[s, my_ta] = part_out[s, :, pl.ds(pl.multiple_of(my_ta * strip, strip), strip), :]

        @pl.when(s > 0)
        def _():
            flows(s - 1)

        return carry

    lax.fori_loop(0, pair_count, couple, 0)
    flows(pair_count - 1)

    for peer in peers:
        remote(acc_first, first_in.at[my_pb], send4.at[0], recv4.at[0], (peer, my_ta)).start()
    for mate in mates:
        remote(acc_second, second_in.at[my_ta], send4.at[1], recv4.at[1], (my_pb, mate)).start()
    first_in[my_pb] = acc_first[...]
    second_in[my_ta] = acc_second[...]
    copy = remote(
        first_in.at[pl.ds(0, n_peers)], first_in.at[pl.ds(0, n_peers)],
        send4.at[0], recv4.at[0], (peers[0], my_ta),
    )
    copy.wait_send()
    copy.wait_recv()
    total[...] = jnp.sum(first_in[...], axis=0)
    for mate in mates:
        remote(total, total_in.at[my_ta], send4.at[2], recv4.at[2], (my_pb, mate)).start()
    total_in[my_ta] = total[...]
    for ref, sem in ((second_in, 1), (total_in, 2)):
        copy = remote(
            ref.at[pl.ds(0, n_mates)], ref.at[pl.ds(0, n_mates)],
            send4.at[sem], recv4.at[sem], (my_pb, mates[0]),
        )
        copy.wait_send()
        copy.wait_recv()
    flow = []
    for c in range(2):
        turn[c] = jnp.transpose(total_in[:, c].reshape(rows, rows))
        mine = turn[c, pl.ds(pl.multiple_of(my_pb * blocks, blocks), blocks), :]
        flow.append(mine + jnp.sum(second_in[:, c], axis=0))
    line_out[...] = flow[0]
    new_out[...] = (source[...] + flow[1]) / (inv_tau[...] + flow[0])


def shards(
    coeffs,
    elph_table,
    energies,
    phonon_energy,
    deviation,
    source,
    inv_tau,
    block_pairs,
    mode_index,
    offsets,
):
    blocks, rows, trans = coeffs.shape
    modes, trans_all = elph_table.shape
    pb_count = lax.axis_size("pb")
    ta_count = lax.axis_size("ta")
    strip = rows // ta_count
    width = trans // pb_count
    low = lax.axis_index("ta") * trans
    ints, values = pair_lists(
        block_pairs, mode_index, offsets, phonon_energy, blocks, low, trans_all
    )
    smem = pl.BlockSpec(memory_space=pltpu.SMEM)
    vmem = pl.BlockSpec(memory_space=pltpu.VMEM)
    f32, bf16 = jnp.float32, jnp.bfloat16
    out = jax.ShapeDtypeStruct((blocks, rows), f32)
    dma = pltpu.SemaphoreType.DMA
    return pl.pallas_call(
        kernel,
        out_shape=(out, out),
        in_specs=[smem, smem] + [vmem] * 6,
        out_specs=(vmem, vmem),
        scratch_shapes=[
            pltpu.VMEM((pb_count * blocks, rows, width), bf16),
            pltpu.VMEM((PAIRS_DEV, pb_count - 1, rows, width), bf16),
            pltpu.VMEM((PAIRS_DEV, rows, trans), bf16),
            pltpu.VMEM((PAIRS_DEV, modes, rows, rows), bf16),
            pltpu.VMEM((PAIRS_DEV, ta_count, modes, strip, rows), bf16),
            pltpu.VMEM((PAIRS_DEV, modes, strip, rows), f32),
            pltpu.VMEM((PAIRS_DEV, modes, strip, rows), f32),
            pltpu.VMEM((PAIRS_DEV, strip, rows), f32),
            pltpu.VMEM(((trans_all + trans) // LANES + 1, 16, LANES), f32),
            pltpu.VMEM((PAIRS_DEV, 16, trans), f32),
            pltpu.VMEM((2, rows, rows), f32),
            pltpu.VMEM((2, strip, rows), f32),
            pltpu.VMEM((2, blocks, rows), f32),
            pltpu.VMEM((pb_count, 2, strip, rows), f32),
            pltpu.VMEM((ta_count, 2, blocks, rows), f32),
            pltpu.VMEM((2, strip, rows), f32),
            pltpu.VMEM((ta_count, 2, strip, rows), f32),
            dma((pb_count - 1,)), dma((pb_count - 1,)),
            dma((PAIRS_DEV,)), dma((PAIRS_DEV,)),
            dma((PAIRS_DEV,)), dma((PAIRS_DEV,)),
            dma((3,)), dma((3,)),
        ],
        compiler_params=pltpu.CompilerParams(
            collective_id=0, has_side_effects=True, vmem_limit_bytes=56 << 20
        ),
        name="rates",
    )(ints, values, coeffs, elph_table, energies, deviation, source, inv_tau)


def solution(mesh):
    in_specs = (
        P("pb", None, "ta"),
        P(),
        P(),
        P(),
        P(),
        P("pb", None),
        P("pb", None),
        P(),
        P(),
        P(),
    )
    out_specs = (P("pb", None), P("pb", None))
    return jax.shard_map(shards, mesh=mesh, in_specs=in_specs, out_specs=out_specs, check_vma=False)
```

time: 842 us -> 159 us (0.19)
  waiting for transfers between devices: 459 us -> 0 us
  Pallas kernels: 0 us -> 149 us
  loops' own time: 97.1 us -> 0 us
  other arithmetic: 95.8 us -> 3.01 us
  matrix products: 79.1 us -> 0 us
  local copies, waits for them, and re-layouts: 74.6 us -> 5.78 us
  starting transfers between devices: 15.5 us -> 0 us
  between operations: 14.3 us -> 0.7 us
    all_to_all x2 -> x0, waiting for transfers between devices: 297 us -> none  [the longest x1 291 us: shards(): lax.all_to_all(send_blocks, 'pb', split_axis=0, concat_axis=0, tiled=True)]
    psum x1 -> x0, waiting for transfers between devices: 162 us -> none  [shards(): coupling = lax.psum(partials, 'ta')]
    pallas_call x0 -> x1, Pallas kernels: none -> 149 us  [shards(): pl.pallas_call(kernel, out_shape=(out, out), in_specs=[smem, smem] + [vme...]
    another operation x2 -> x0, loops' own time: 97.1 us -> none  [the longest x1 95.9 us: shards(): lax.map(lambda pair_item: couple(pair_item, state_rows), item_arrays)]
    dot_general x27 -> x0, matrix products: 79.1 us -> none  [the longest x24 78.5 us: couple(): lax.dot_general(scaled.reshape(mode_count * row_count, trans_local), coef...]
    mul x49 -> x0, other arithmetic: 63.8 us -> none  [the longest x24 36.5 us: pair_rates(): strength * ((occupation + 1.0) * lorentz_plus + occupation * lorentz_minus)]
    dynamic_slice x96 -> x0, local copies, waits for them, and re-layouts: 44.1 us -> none  [the longest x72 41.9 us: shards(): lax.map(lambda pair_item: couple(pair_item, state_rows), item_arrays)]
    gather x29 -> x0, local copies, waits for them, and re-layouts: 25.5 us -> none  [the longest x24 13.9 us: couple(): coupling_table = jnp.take(window, mode_rows, axis=0)]
  transfers between devices with their start and end apart: 3 -> 0, of which waited for: 3 -> 0; matrix products, arithmetic and copies ran while one was open for 0% -> 0% of each run, Pallas kernels for 0% -> 0%
where the time goes in v1:
time: 159 us
  Pallas kernels  149 us (94%)
  local copies, waits for them, and re-layouts  5.78 us (4%)
  other arithmetic  3.01 us (2%)
    pallas_call x1, Pallas kernels, shards(): pl.pallas_call(kernel, out_shape=(out, out), in_specs=[smem, smem] + [vme...  149 us

profile of v1, /device:TPU:1, one launch (start us, length us, event | category | flops | bytes accessed | tf_op | source)
XLA Modules:
  0.0 159.0 jit_solution(12619068470395746163)
XLA Ops:
  0.6 0.7 and_select_fusion
  1.3 0.7 negate_select_fusion
  2.0 1.5 concatenate.7
  3.5 0.2 convert_reduce_fusion
  3.8 0.6 select_reduce_fusion
  4.4 0.1 copy.16
  4.5 0.8 reshape.73.ints
  5.3 0.8 select_reduce_fusion.1
  6.1 0.1 copy.17
  6.2 0.7 reshape.74.values
  6.9 149.5 %rates.1 = (f32[8,128]{1,0:T(8,128)}, f32[8,128]{1,0:T(8,128)}) custom-call(s32[960]{0:T(1024)} %reshape.73.ints, f32[3456]{0:T(1024)} %reshape.74.values, bf16[8,128,2048]{2,1,0:T(8,128)(2,1)} %coeffs.1, bf16[9,16384]{1,0:T(8,128)(2,1)} %table.1, f32[128,128]{1,0:T(8,128)} %energies.1, f32[128,128]{1,0:T(8,128)} %deviation.1, f32[8,128]{1,0:T(8,128)} %source.1, ...), custom_call_target="tpu_custom_call" | custom-call | tf_op jit(solution)/shard_map/rates/pallas_call | solution.py:281
  156.4 1.3 copy.20
  157.7 1.3 copy.21
  (8 shorter events, 0.1 us)

commit v2 on v1

v2 whole, which is shorter than its diff:
```python
import jax
import jax.numpy as jnp
from jax import lax
from jax.experimental import pallas as pl
from jax.experimental.pallas import tpu as pltpu
from jax.sharding import PartitionSpec as P

PAIRS_DEV = 12
BOLTZMANN_KT = 0.02585
BROADENING = 0.01
MESH = pl.DeviceIdType.MESH
LANES = 128
TILE = 16
HALVES = 2
ROUND = 2
FIRST, SECOND, PLACE, START, SHIFT, MODE = range(6)

MOVES = (
    (1, 0), (0, 1), (3, 0), (0, 3), (1, 1), (3, 3), (1, 3), (3, 1),
    (2, 0), (0, 2), (2, 1), (1, 2), (2, 3), (3, 2), (2, 2),
)


def kernel(
    phonon, coeffs, table, energies, deviation, block_pairs, mode_index, offsets,
    flow_out,
    held, pieces_a, pieces_b, stage, other, scaled, part_out, part_in,
    weight_f, weight_b, value_a, wide, window, turn, lists, ints,
    acc_first, acc_second, first_out, first_in, second_in, total, total_in,
    local, send1, recv1, send2, recv2, send3, recv3, send4, recv4,
):
    blocks, rows, trans = coeffs.shape
    modes, trans_all = table.shape
    pair_total = block_pairs.shape[0]
    pair_count = other.shape[0]
    my_pb = lax.axis_index("pb")
    my_ta = lax.axis_index("ta")
    ta_count = part_in.shape[1]
    half = rows // HALVES
    strip = half // ta_count
    rounds = pair_count // ROUND
    my_y, my_z = my_pb // 4, my_pb % 4
    peers = [((my_y + dy) % 4) * 4 + (my_z + dz) % 4 for dy, dz in MOVES]
    mates = [(my_ta + d) % ta_count for d in range(1, ta_count)]
    n_peers, n_mates = len(peers), len(mates)
    pieces = (pieces_a, pieces_b)

    barrier = pltpu.get_barrier_semaphore()
    for peer in peers:
        pl.semaphore_signal(barrier, inc=1, device_id=(peer, my_ta), device_id_type=MESH)
    for mate in mates:
        pl.semaphore_signal(barrier, inc=1, device_id=(my_pb, mate), device_id_type=MESH)
    fetch = pltpu.make_async_copy(coeffs, held, local.at[0])
    fetch.start()
    pl.semaphore_wait(barrier, n_peers + n_mates)

    def remote(src, dst, send, recv, device):
        return pltpu.make_async_remote_copy(
            src_ref=src, dst_ref=dst, send_sem=send, recv_sem=recv,
            device_id=device, device_id_type=MESH,
        )

    my_lane = pl.multiple_of(my_pb * LANES, LANES)
    for h in range(HALVES):
        def spread(g, carry, h=h):
            for k, peer in enumerate(peers):
                lane = pl.multiple_of(peer * LANES, LANES)
                remote(
                    coeffs.at[pl.ds(ROUND * g, ROUND), pl.ds(h * half, half), pl.ds(lane, LANES)],
                    pieces[h].at[pl.ds(my_pb * blocks + ROUND * g, ROUND)],
                    send1.at[h, k], recv1.at[h, k], (peer, my_ta),
                ).start()
            return carry

        lax.fori_loop(0, blocks // ROUND, spread, 0)

    shift_of = blocks.bit_length() - 1
    second = block_pairs[:, 1:2]
    owner = lax.shift_right_logical(second, shift_of)
    serial = lax.broadcasted_iota(jnp.int32, (pair_total, LANES), 0)
    mine = (lax.broadcasted_iota(jnp.int32, (pair_total, LANES), 1) == owner).astype(jnp.int32)
    count = mine
    step = 1
    while step < pair_total:
        count = count + jnp.where(serial >= step, pltpu.roll(count, step, 0), 0)
        step *= 2
    rank = jnp.sum(mine * (count - 1), axis=1, keepdims=True)
    slot = owner * pair_count + rank
    spread_lanes = lists.shape[1]
    hot = lax.broadcasted_iota(jnp.int32, (pair_total, spread_lanes), 1) == slot
    lists[...] = jnp.zeros_like(lists)
    lists[0:1, 0:pair_total] = offsets[...]
    offset = jnp.transpose(jnp.broadcast_to(lists[0:1, :], (LANES, spread_lanes)))
    offset = offset[:pair_total, 0:1]
    start = offset + my_ta * trans
    start = jnp.where(start >= trans_all, start - trans_all, start)
    columns = [
        block_pairs[:, 0:1], second, second & (blocks - 1),
        lax.shift_right_logical(start, 7), start & (LANES - 1),
    ] + [mode_index[:, m:m + 1] for m in range(modes)]
    for c, column in enumerate(columns):
        lists[c:c + 1, :] = jnp.sum(jnp.where(hot, column, 0), axis=0, keepdims=True)
    listing = pltpu.make_async_copy(lists, ints, local.at[1])
    listing.start()
    fetch.wait()
    listing.wait()
    for h in range(HALVES):
        pieces[h][pl.ds(my_pb * blocks, blocks)] = held[:, pl.ds(h * half, half), pl.ds(my_lane, LANES)]

    def number(s, which):
        return ints[which, my_pb * pair_count + s]

    def hand_on(h):
        for k, peer in enumerate(peers):
            lane = pl.multiple_of(peer * LANES, LANES)
            copy = remote(
                coeffs.at[:, pl.ds(h * half, half), pl.ds(lane, LANES)],
                pieces[h].at[pl.ds(my_pb * blocks, blocks)],
                send1.at[h, k], recv1.at[h, k], (peer, my_ta),
            )
            copy.wait_send()
            copy.wait_recv()

        def deliver(g, carry):
            for k, peer in enumerate(peers):
                for u in range(ROUND):
                    stage[h, g, k, u] = pieces[h][ints[FIRST, peer * pair_count + ROUND * g + u]]
                remote(
                    stage.at[h, g, k],
                    other.at[pl.ds(ROUND * g, ROUND), pl.ds(h * half, half), pl.ds(my_lane, LANES)],
                    send2.at[h, g], recv2.at[h, g], (peer, my_ta),
                ).start()
            for u in range(ROUND):
                other[ROUND * g + u, pl.ds(h * half, half), pl.ds(my_lane, LANES)] = (
                    pieces[h][number(ROUND * g + u, FIRST)]
                )
            return carry

        lax.fori_loop(0, rounds, deliver, 0)

    hand_on(0)

    wide[...] = jnp.zeros_like(wide)
    tiles_all = trans_all // LANES
    tiles = trans // LANES

    def widen(tile, carry):
        lane = pl.multiple_of(lax.rem(tile, tiles_all) * LANES, LANES)
        wide[tile, pl.ds(0, modes), :] = table[:, pl.ds(lane, LANES)].astype(jnp.float32)
        return carry

    lax.fori_loop(0, wide.shape[0], widen, 0)
    acc_first[...] = jnp.zeros_like(acc_first)
    acc_second[...] = jnp.zeros_like(acc_second)

    def strips_of(source_ref, block):
        row = source_ref[pl.ds(block, 1), :]
        turn[...] = jnp.transpose(jnp.broadcast_to(row, (rows, rows)))
        return [
            turn[pl.ds(pl.multiple_of(h * half + my_ta * strip, strip), strip), :]
            for h in range(HALVES)
        ]

    def prepare(s, carry):
        first, second_one = number(s, FIRST), number(s, SECOND)
        piece = wide[pl.ds(number(s, START), tiles + 1)]
        amount = jnp.full(piece.shape, number(s, SHIFT), jnp.int32)
        for bit in range(7):
            moved = pltpu.roll(piece, LANES - (1 << bit), 2)
            piece = jnp.where((amount & (1 << bit)) != 0, moved, piece)
        keep = lax.broadcasted_iota(jnp.int32, (TILE, LANES), 1) < LANES - amount[0]
        for t in range(tiles):
            window[s, :, t * LANES:(t + 1) * LANES] = jnp.where(keep, piece[t], piece[t + 1])
        energy_b = energies[pl.ds(second_one, 1), :]
        energy_a = strips_of(energies, first)
        for h in range(HALVES):
            detuning = energy_a[h] - energy_b
            for m in range(modes):
                energy = jnp.full(detuning.shape, phonon[m], jnp.float32)
                bose = 1.0 / (jnp.exp(energy / BOLTZMANN_KT) - 1.0)
                minus = 1.0 / (1.0 + ((detuning - energy) / BROADENING) ** 2)
                plus = 1.0 / (1.0 + ((detuning + energy) / BROADENING) ** 2)
                scale = 1.0 / (modes * rows)
                weight_f[s, h, m] = ((bose + 1.0) * minus + bose * plus) * scale
                weight_b[s, h, m] = ((bose + 1.0) * plus + bose * minus) * scale
        for h, value in enumerate(strips_of(deviation, first)):
            value_a[s, h] = value
        return carry

    lax.fori_loop(0, pair_count, prepare, 0)
    for h in range(1, HALVES):
        hand_on(h)

    def flows(h, s):
        index = h * pair_count + s
        copy = remote(
            part_in.at[index, pl.ds(0, n_mates)], part_in.at[index, pl.ds(0, n_mates)],
            send3.at[index], recv3.at[index], (my_pb, mates[0]),
        )
        copy.wait_send()
        copy.wait_recv()
        coupling = part_in[index, 0].astype(jnp.float32)
        for q in range(1, ta_count):
            coupling = coupling + part_in[index, q].astype(jnp.float32)
        coupling = coupling[:modes * strip].reshape(modes, strip, rows)
        square = coupling * coupling
        forward = jnp.sum(square * weight_f[s, h], axis=0)
        backward = jnp.sum(square * weight_b[s, h], axis=0)
        value_b = deviation[pl.ds(number(s, SECOND), 1), :]
        out_first = jnp.sum(forward, axis=1, keepdims=True)
        in_first = jnp.sum(backward * value_b, axis=1, keepdims=True)
        out_second = jnp.sum(backward, axis=0, keepdims=True)
        in_second = jnp.sum(forward * value_a[s, h], axis=0, keepdims=True)
        here = lax.broadcasted_iota(jnp.int32, (strip, rows), 1) == number(s, FIRST)
        acc_first[0, h] += jnp.where(here, out_first, 0.0)
        acc_first[1, h] += jnp.where(here, in_first, 0.0)
        there = lax.broadcasted_iota(jnp.int32, (blocks, rows), 0) == number(s, PLACE)
        acc_second[0] += jnp.where(there, out_second, 0.0)
        acc_second[1] += jnp.where(there, in_second, 0.0)

    pad = part_out.shape[2] - modes * strip

    def couple(n, carry):
        h, g = n // rounds, n % rounds
        copy = remote(
            stage.at[h, g], stage.at[h, g], send2.at[h, g], recv2.at[h, g], (peers[0], my_ta),
        )
        copy.wait_send()
        copy.wait_recv()
        for u in range(ROUND):
            s = ROUND * g + u
            index = h * pair_count + s
            block = other[s, pl.ds(pl.multiple_of(h * half, half), half), :]
            block = block.reshape(half // TILE, TILE, trans)
            for m in range(modes):
                row = window[s, pl.ds(number(s, MODE + m), 1), :]
                scale = jnp.broadcast_to(row, (TILE, trans)).astype(jnp.bfloat16)
                scaled[m * half:(m + 1) * half, :] = (block * scale[None]).reshape(half, trans)
            product = lax.dot_general(
                scaled[...], held[number(s, PLACE)],
                (((1,), (1,)), ((), ())), preferred_element_type=jnp.float32,
            ).reshape(modes, ta_count, strip, rows)
            for q in range(ta_count):
                part = jnp.concatenate(
                    [product[:, q].reshape(modes * strip, rows), jnp.zeros((pad, rows), jnp.float32)], axis=0
                )
                part_out[index, q] = part.astype(jnp.bfloat16)
            for mate in mates:
                remote(
                    part_out.at[index, mate], part_in.at[index, my_ta],
                    send3.at[index], recv3.at[index], (my_pb, mate),
                ).start()
            part_in[index, my_ta] = part_out[index, my_ta]

        @pl.when(n > 0)
        def _():
            before_h, before_g = (n - 1) // rounds, (n - 1) % rounds
            for u in range(ROUND):
                flows(before_h, ROUND * before_g + u)

        return carry

    lax.fori_loop(0, HALVES * rounds, couple, 0)
    for u in range(ROUND):
        flows(HALVES - 1, pair_count - ROUND + u)

    used = 2 * HALVES * strip
    stacked = jnp.concatenate(
        [acc_first[...].reshape(used, rows), jnp.zeros((LANES - used, rows), jnp.float32)], axis=0
    )
    first_out[...] = jnp.transpose(stacked)
    for peer in peers:
        remote(
            first_out.at[pl.ds(pl.multiple_of(peer * blocks, blocks), blocks)], first_in.at[my_pb],
            send4.at[0], recv4.at[0], (peer, my_ta),
        ).start()
    for mate in mates:
        remote(acc_second, second_in.at[my_ta], send4.at[1], recv4.at[1], (my_pb, mate)).start()
    first_in[my_pb] = first_out[pl.ds(pl.multiple_of(my_pb * blocks, blocks), blocks)]
    second_in[my_ta] = acc_second[...]
    copy = remote(
        first_in.at[pl.ds(0, n_peers)], first_in.at[pl.ds(0, n_peers)],
        send4.at[0], recv4.at[0], (peers[0], my_ta),
    )
    copy.wait_send()
    copy.wait_recv()
    total[...] = jnp.sum(first_in[...], axis=0)
    for mate in mates:
        remote(total, total_in.at[my_ta], send4.at[2], recv4.at[2], (my_pb, mate)).start()
    total_in[my_ta] = total[...]
    for ref, sem in ((second_in, 1), (total_in, 2)):
        copy = remote(
            ref.at[pl.ds(0, n_mates)], ref.at[pl.ds(0, n_mates)],
            send4.at[sem], recv4.at[sem], (my_pb, mates[0]),
        )
        copy.wait_send()
        copy.wait_recv()
    lane = lax.broadcasted_iota(jnp.int32, (blocks, LANES), 1)
    for c in range(2):
        flow = jnp.sum(second_in[:, c], axis=0)
        for h in range(HALVES):
            low = (c * HALVES + h) * strip
            inside = (lane >= low) & (lane < low + strip)
            for q in range(ta_count):
                target = h * half + q * strip
                part = jnp.where(inside, total_in[q], 0.0)
                flow = flow + pltpu.roll(part, (target - low) % LANES, 1)
        flow_out[c] = flow


def shards(
    coeffs,
    elph_table,
    energies,
    phonon_energy,
    deviation,
    source,
    inv_tau,
    block_pairs,
    mode_index,
    offsets,
):
    blocks, rows, trans = coeffs.shape
    modes, trans_all = elph_table.shape
    pair_total = block_pairs.shape[0]
    pb_count = lax.axis_size("pb")
    ta_count = lax.axis_size("ta")
    half = rows // HALVES
    strip = half // ta_count
    rounds = PAIRS_DEV // ROUND
    units = HALVES * PAIRS_DEV
    padded = -(-modes * strip // TILE) * TILE
    list_lanes = -(-pair_total // LANES) * LANES
    smem = pl.BlockSpec(memory_space=pltpu.SMEM)
    vmem = pl.BlockSpec(memory_space=pltpu.VMEM)
    f32, bf16 = jnp.float32, jnp.bfloat16
    dma = pltpu.SemaphoreType.DMA
    flow = pl.pallas_call(
        kernel,
        out_shape=jax.ShapeDtypeStruct((2, blocks, rows), f32),
        in_specs=[smem, pl.BlockSpec(memory_space=pl.ANY)] + [vmem] * 6,
        out_specs=vmem,
        scratch_shapes=[
            pltpu.VMEM((blocks, rows, trans), bf16),
            pltpu.VMEM((pb_count * blocks, half, LANES), bf16),
            pltpu.VMEM((pb_count * blocks, half, LANES), bf16),
            pltpu.VMEM((HALVES, rounds, pb_count - 1, ROUND, half, LANES), bf16),
            pltpu.VMEM((PAIRS_DEV, rows, trans), bf16),
            pltpu.VMEM((modes * half, trans), bf16),
            pltpu.VMEM((units, ta_count, padded, rows), bf16),
            pltpu.VMEM((units, ta_count, padded, rows), bf16),
            pltpu.VMEM((PAIRS_DEV, HALVES, modes, strip, rows), f32),
            pltpu.VMEM((PAIRS_DEV, HALVES, modes, strip, rows), f32),
            pltpu.VMEM((PAIRS_DEV, HALVES, strip, rows), f32),
            pltpu.VMEM(((trans_all + trans) // LANES + 1, TILE, LANES), f32),
            pltpu.VMEM((PAIRS_DEV, TILE, trans), f32),
            pltpu.VMEM((rows, rows), f32),
            pltpu.VMEM((TILE, list_lanes), jnp.int32),
            pltpu.SMEM((TILE, list_lanes), jnp.int32),
            pltpu.VMEM((2, HALVES, strip, rows), f32),
            pltpu.VMEM((2, blocks, rows), f32),
            pltpu.VMEM((pb_count * blocks, LANES), f32),
            pltpu.VMEM((pb_count, blocks, LANES), f32),
            pltpu.VMEM((ta_count, 2, blocks, rows), f32),
            pltpu.VMEM((blocks, LANES), f32),
            pltpu.VMEM((ta_count, blocks, LANES), f32),
            dma((2,)),
            dma((HALVES, pb_count - 1)), dma((HALVES, pb_count - 1)),
            dma((HALVES, rounds)), dma((HALVES, rounds)),
            dma((units,)), dma((units,)),
            dma((3,)), dma((3,)),
        ],
        compiler_params=pltpu.CompilerParams(
            collective_id=0, has_side_effects=True, vmem_limit_bytes=56 << 20
        ),
        name="rates",
    )(
        phonon_energy, coeffs, elph_table, energies, deviation, block_pairs, mode_index,
        offsets.reshape(1, pair_total),
    )
    return (source + flow[1]) / (inv_tau + flow[0]), flow[0]


def solution(mesh):
    in_specs = (
        P("pb", None, "ta"),
        P(),
        P(),
        P(),
        P(),
        P("pb", None),
        P("pb", None),
        P(),
        P(),
        P(),
    )
    out_specs = (P("pb", None), P("pb", None))
    return jax.shard_map(shards, mesh=mesh, in_specs=in_specs, out_specs=out_specs, check_vma=False)
```

time: 159 us -> 149 us (0.937)
  Pallas kernels: 149 us -> 144 us
  local copies, waits for them, and re-layouts: 5.78 us -> 2.9 us
  other arithmetic: 3.01 us -> 1.29 us
    pallas_call x1, Pallas kernels: 149 us -> 144 us  [shards(): pl.pallas_call(kernel, out_shape=jax.ShapeDtypeStruct((2, blocks, rows),...]
    concatenate x2 -> x0, local copies, waits for them, and re-layouts: 1.59 us -> none  [the longest x1 1.48 us: pair_lists(): data = jnp.concatenate([jnp.stack(columns, axis=1), mode_index], axis=1)]
where the time goes in v2:
time: 149 us
  Pallas kernels  144 us (97%)
  local copies, waits for them, and re-layouts  2.9 us (2%)
    pallas_call x1, Pallas kernels, shards(): pl.pallas_call(kernel, out_shape=jax.ShapeDtypeStruct((2, blocks, rows),...  144 us

profile of v2, /device:TPU:1, one launch (start us, length us, event | category | flops | bytes accessed | tf_op | source)
XLA Modules:
  0.0 148.6 jit_solution(4805094162815699650)
XLA Ops:
  0.6 0.0 copy-start.1
  0.6 0.0 copy-start
  0.7 1.4 copy.12.block_pairs
  2.1 1.5 copy.13.mode_index
  3.5 143.8 %rates.1 = f32[2,8,128]{2,1,0:T(8,128)} custom-call(f32[9]{0:T(128)} %phonon.1, bf16[8,128,2048]{2,1,0:T(8,128)(2,1)} %coeffs.1, bf16[9,16384]{1,0:T(8,128)(2,1)} %table.1, f32[128,128]{1,0:T(8,128)} %energies.1, f32[128,128]{1,0:T(8,128)} %deviation.1, s32[192,2]{1,0:T(8,128)} %copy.12.block_pairs, s32[192,9]{1,0:T(8,128)} %copy.13.mode_index, s32[1,192]{1,0:T(1,128)} %bitcast.8), custom_call_target="tpu_custom_call" | custom-call | tf_op jit(solution)/shard_map/rates/pallas_call | solution.py:338
  147.3 0.0 copy-done.1
  147.3 0.0 copy-done
  147.3 1.3 fusion
Async XLA Ops:
  0.6 146.7 %copy-start.1 = (f32[8,128]{1,0:T(8,128)S(1)}, f32[8,128]{1,0:T(8,128)}, u32[]{:S(2)}) copy-start(f32[8,128]{1,0:T(8,128)} %param.16) | copy-start | bytes 12292
  0.6 146.7 %copy-start = (f32[8,128]{1,0:T(8,128)S(1)}, f32[8,128]{1,0:T(8,128)}, u32[]{:S(2)}) copy-start(f32[8,128]{1,0:T(8,128)} %param.15) | copy-start | bytes 12292

commit v3 on v2

--- a/solution.py
+++ b/solution.py
@@ -16,9 +16,14 @@
 FIRST, SECOND, PLACE, START, SHIFT, MODE = range(6)
 
 MOVES = (
-    (1, 0), (0, 1), (3, 0), (0, 3), (1, 1), (3, 3), (1, 3), (3, 1),
-    (2, 0), (0, 2), (2, 1), (1, 2), (2, 3), (3, 2), (2, 2),
+    (1, 0), (0, 1), (2, 2), (3, 0), (0, 3), (2, 1), (1, 1), (1, 2),
+    (3, 3), (2, 3), (1, 3), (3, 2), (3, 1), (2, 0), (0, 2),
 )
+FAR_MOVES = (
+    (2, 2), (2, 1), (1, 2), (2, 3), (3, 2), (1, 1), (3, 3), (1, 3),
+    (3, 1), (2, 0), (0, 2), (1, 0), (0, 1), (3, 0), (0, 3),
+)
+MATES = (4, 3, 5, 2, 6, 1, 7)
 
 
 def kernel(
@@ -31,17 +36,18 @@
 ):
     blocks, rows, trans = coeffs.shape
     modes, trans_all = table.shape
-    pair_total = block_pairs.shape[0]
-    pair_count = other.shape[0]
+    pair_total = block_pairs.shape[1]
+    rounds = other.shape[1]
+    pair_count = rounds * ROUND
     my_pb = lax.axis_index("pb")
     my_ta = lax.axis_index("ta")
     ta_count = part_in.shape[1]
     half = rows // HALVES
     strip = half // ta_count
-    rounds = pair_count // ROUND
     my_y, my_z = my_pb // 4, my_pb % 4
     peers = [((my_y + dy) % 4) * 4 + (my_z + dz) % 4 for dy, dz in MOVES]
-    mates = [(my_ta + d) % ta_count for d in range(1, ta_count)]
+    far_peers = [((my_y + dy) % 4) * 4 + (my_z + dz) % 4 for dy, dz in FAR_MOVES]
+    mates = [(my_ta + d) % ta_count for d in MATES]
     n_peers, n_mates = len(peers), len(mates)
     pieces = (pieces_a, pieces_b)
 
@@ -75,7 +81,13 @@
         lax.fori_loop(0, blocks // ROUND, spread, 0)
 
     shift_of = blocks.bit_length() - 1
-    second = block_pairs[:, 1:2]
+    spread_lanes = lists.shape[1]
+    lists[...] = jnp.zeros_like(lists)
+    lists[0:2, 0:pair_total] = block_pairs[...]
+    lists[2:3, 0:pair_total] = offsets[...]
+    lists[MODE:MODE + modes, 0:pair_total] = mode_index[...]
+    column_form = jnp.transpose(lists[...])[:pair_total]
+    second = column_form[:, 1:2]
     owner = lax.shift_right_logical(second, shift_of)
     serial = lax.broadcasted_iota(jnp.int32, (pair_total, LANES), 0)
     mine = (lax.broadcasted_iota(jnp.int32, (pair_total, LANES), 1) == owner).astype(jnp.int32)
@@ -86,21 +98,16 @@
         step *= 2
     rank = jnp.sum(mine * (count - 1), axis=1, keepdims=True)
     slot = owner * pair_count + rank
-    spread_lanes = lists.shape[1]
     hot = lax.broadcasted_iota(jnp.int32, (pair_total, spread_lanes), 1) == slot
-    lists[...] = jnp.zeros_like(lists)
-    lists[0:1, 0:pair_total] = offsets[...]
-    offset = jnp.transpose(jnp.broadcast_to(lists[0:1, :], (LANES, spread_lanes)))
-    offset = offset[:pair_total, 0:1]
-    start = offset + my_ta * trans
+    start = column_form[:, 2:3] + my_ta * trans
     start = jnp.where(start >= trans_all, start - trans_all, start)
     columns = [
-        block_pairs[:, 0:1], second, second & (blocks - 1),
+        column_form[:, 0:1], second, second & (blocks - 1),
         lax.shift_right_logical(start, 7), start & (LANES - 1),
-    ] + [mode_index[:, m:m + 1] for m in range(modes)]
+    ] + [column_form[:, MODE + m:MODE + m + 1] for m in range(modes)]
     for c, column in enumerate(columns):
         lists[c:c + 1, :] = jnp.sum(jnp.where(hot, column, 0), axis=0, keepdims=True)
-    listing = pltpu.make_async_copy(lists, ints, local.at[1])
+    listing = pltpu.make_async_copy(lists.at[pl.ds(0, TILE)], ints, local.at[1])
     listing.start()
     fetch.wait()
     listing.wait()
@@ -118,7 +125,6 @@
                 pieces[h].at[pl.ds(my_pb * blocks, blocks)],
                 send1.at[h, k], recv1.at[h, k], (peer, my_ta),
             )
-            copy.wait_send()
             copy.wait_recv()
 
         def deliver(g, carry):
@@ -127,13 +133,11 @@
                     stage[h, g, k, u] = pieces[h][ints[FIRST, peer * pair_count + ROUND * g + u]]
                 remote(
                     stage.at[h, g, k],
-                    other.at[pl.ds(ROUND * g, ROUND), pl.ds(h * half, half), pl.ds(my_lane, LANES)],
+                    other.at[h, g, my_pb],
                     send2.at[h, g], recv2.at[h, g], (peer, my_ta),
                 ).start()
             for u in range(ROUND):
-                other[ROUND * g + u, pl.ds(h * half, half), pl.ds(my_lane, LANES)] = (
-                    pieces[h][number(ROUND * g + u, FIRST)]
-                )
+                other[h, g, my_pb, u] = pieces[h][number(ROUND * g + u, FIRST)]
             return carry
 
         lax.fori_loop(0, rounds, deliver, 0)
@@ -197,7 +201,6 @@
             part_in.at[index, pl.ds(0, n_mates)], part_in.at[index, pl.ds(0, n_mates)],
             send3.at[index], recv3.at[index], (my_pb, mates[0]),
         )
-        copy.wait_send()
         copy.wait_recv()
         coupling = part_in[index, 0].astype(jnp.float32)
         for q in range(1, ta_count):
@@ -220,22 +223,31 @@
 
     pad = part_out.shape[2] - modes * strip
 
+    def flows_of(n):
+        for u in range(ROUND):
+            flows(n // rounds, ROUND * (n % rounds) + u)
+
     def couple(n, carry):
         h, g = n // rounds, n % rounds
+
+        @pl.when(n > 1)
+        def _():
+            flows_of(n - 2)
+
         copy = remote(
             stage.at[h, g], stage.at[h, g], send2.at[h, g], recv2.at[h, g], (peers[0], my_ta),
         )
-        copy.wait_send()
         copy.wait_recv()
         for u in range(ROUND):
             s = ROUND * g + u
             index = h * pair_count + s
-            block = other[s, pl.ds(pl.multiple_of(h * half, half), half), :]
-            block = block.reshape(half // TILE, TILE, trans)
             for m in range(modes):
                 row = window[s, pl.ds(number(s, MODE + m), 1), :]
                 scale = jnp.broadcast_to(row, (TILE, trans)).astype(jnp.bfloat16)
-                scaled[m * half:(m + 1) * half, :] = (block * scale[None]).reshape(half, trans)
+                for t in range(tiles):
+                    block = other[h, g, t, u].reshape(half // TILE, TILE, LANES)
+                    block = block * scale[None, :, t * LANES:(t + 1) * LANES]
+                    scaled[m * half:(m + 1) * half, t * LANES:(t + 1) * LANES] = block.reshape(half, LANES)
             product = lax.dot_general(
                 scaled[...], held[number(s, PLACE)],
                 (((1,), (1,)), ((), ())), preferred_element_type=jnp.float32,
@@ -251,25 +263,18 @@
                     send3.at[index], recv3.at[index], (my_pb, mate),
                 ).start()
             part_in[index, my_ta] = part_out[index, my_ta]
-
-        @pl.when(n > 0)
-        def _():
-            before_h, before_g = (n - 1) // rounds, (n - 1) % rounds
-            for u in range(ROUND):
-                flows(before_h, ROUND * before_g + u)
-
         return carry
 
     lax.fori_loop(0, HALVES * rounds, couple, 0)
-    for u in range(ROUND):
-        flows(HALVES - 1, pair_count - ROUND + u)
+    for n in range(HALVES * rounds - 2, HALVES * rounds):
+        flows_of(n)
 
     used = 2 * HALVES * strip
     stacked = jnp.concatenate(
         [acc_first[...].reshape(used, rows), jnp.zeros((LANES - used, rows), jnp.float32)], axis=0
     )
     first_out[...] = jnp.transpose(stacked)
-    for peer in peers:
+    for peer in far_peers:
         remote(
             first_out.at[pl.ds(pl.multiple_of(peer * blocks, blocks), blocks)], first_in.at[my_pb],
             send4.at[0], recv4.at[0], (peer, my_ta),
@@ -278,21 +283,40 @@
         remote(acc_second, second_in.at[my_ta], send4.at[1], recv4.at[1], (my_pb, mate)).start()
     first_in[my_pb] = first_out[pl.ds(pl.multiple_of(my_pb * blocks, blocks), blocks)]
     second_in[my_ta] = acc_second[...]
-    copy = remote(
-        first_in.at[pl.ds(0, n_peers)], first_in.at[pl.ds(0, n_peers)],
-        send4.at[0], recv4.at[0], (peers[0], my_ta),
-    )
-    copy.wait_send()
-    copy.wait_recv()
+
+    for h in range(HALVES):
+        for k, peer in enumerate(peers):
+            lane = pl.multiple_of(peer * LANES, LANES)
+            remote(
+                coeffs.at[:, pl.ds(h * half, half), pl.ds(lane, LANES)],
+                pieces[h].at[pl.ds(my_pb * blocks, blocks)],
+                send1.at[h, k], recv1.at[h, k], (peer, my_ta),
+            ).wait_send()
+
+    def sent(n, carry):
+        h, g = n // rounds, n % rounds
+        remote(
+            stage.at[h, g], stage.at[h, g], send2.at[h, g], recv2.at[h, g], (peers[0], my_ta),
+        ).wait_send()
+        for u in range(ROUND):
+            index = ROUND * n + u
+            block = part_in.at[index, pl.ds(0, n_mates)]
+            remote(block, block, send3.at[index], recv3.at[index], (my_pb, mates[0])).wait_send()
+        return carry
+
+    lax.fori_loop(0, HALVES * rounds, sent, 0)
+
+    few = first_in.at[pl.ds(0, n_peers)]
+    sums = remote(few, few, send4.at[0], recv4.at[0], (peers[0], my_ta))
+    sums.wait_recv()
     total[...] = jnp.sum(first_in[...], axis=0)
     for mate in mates:
         remote(total, total_in.at[my_ta], send4.at[2], recv4.at[2], (my_pb, mate)).start()
     total_in[my_ta] = total[...]
+    sums.wait_send()
     for ref, sem in ((second_in, 1), (total_in, 2)):
-        copy = remote(
-            ref.at[pl.ds(0, n_mates)], ref.at[pl.ds(0, n_mates)],
-            send4.at[sem], recv4.at[sem], (my_pb, mates[0]),
-        )
+        few = ref.at[pl.ds(0, n_mates)]
+        copy = remote(few, few, send4.at[sem], recv4.at[sem], (my_pb, mates[0]))
         copy.wait_send()
         copy.wait_recv()
     lane = lax.broadcasted_iota(jnp.int32, (blocks, LANES), 1)
@@ -345,7 +369,7 @@
             pltpu.VMEM((pb_count * blocks, half, LANES), bf16),
             pltpu.VMEM((pb_count * blocks, half, LANES), bf16),
             pltpu.VMEM((HALVES, rounds, pb_count - 1, ROUND, half, LANES), bf16),
-            pltpu.VMEM((PAIRS_DEV, rows, trans), bf16),
+            pltpu.VMEM((HALVES, rounds, pb_count, ROUND, half, LANES), bf16),
             pltpu.VMEM((modes * half, trans), bf16),
             pltpu.VMEM((units, ta_count, padded, rows), bf16),
             pltpu.VMEM((units, ta_count, padded, rows), bf16),
@@ -355,7 +379,7 @@
             pltpu.VMEM(((trans_all + trans) // LANES + 1, TILE, LANES), f32),
             pltpu.VMEM((PAIRS_DEV, TILE, trans), f32),
             pltpu.VMEM((rows, rows), f32),
-            pltpu.VMEM((TILE, list_lanes), jnp.int32),
+            pltpu.VMEM((LANES, list_lanes), jnp.int32),
             pltpu.SMEM((TILE, list_lanes), jnp.int32),
             pltpu.VMEM((2, HALVES, strip, rows), f32),
             pltpu.VMEM((2, blocks, rows), f32),
@@ -375,7 +399,7 @@
         ),
         name="rates",
     )(
-        phonon_energy, coeffs, elph_table, energies, deviation, block_pairs, mode_index,
+        phonon_energy, coeffs, elph_table, energies, deviation, block_pairs.T, mode_index.T,
         offsets.reshape(1, pair_total),
     )
     return (source + flow[1]) / (inv_tau + flow[0]), flow[0]

time: 149 us -> 144 us (0.966)
  local copies, waits for them, and re-layouts: 2.9 us -> 0.01 us
  Pallas kernels: 144 us -> 142 us
    unnamed x6 -> x4, local copies, waits for them, and re-layouts: 2.9 us -> 0.01 us
    pallas_call x1, Pallas kernels: 144 us -> 142 us  [shards(): pl.pallas_call(kernel, out_shape=jax.ShapeDtypeStruct((2, blocks, rows),...]
where the time goes in v3:
time: 144 us
  Pallas kernels  142 us (99%)
    pallas_call x1, Pallas kernels, shards(): pl.pallas_call(kernel, out_shape=jax.ShapeDtypeStruct((2, blocks, rows),...  142 us

profile of v3, /device:TPU:1, one launch (start us, length us, event | category | flops | bytes accessed | tf_op | source)
XLA Modules:
  0.0 143.8 jit_solution(14398477201612231400)
XLA Ops:
  0.6 0.0 copy-start.1
  0.6 0.0 copy-start
  0.7 141.9 %rates.1 = f32[2,8,128]{2,1,0:T(8,128)} custom-call(f32[9]{0:T(128)} %phonon.1, bf16[8,128,2048]{2,1,0:T(8,128)(2,1)} %coeffs.1, bf16[9,16384]{1,0:T(8,128)(2,1)} %table.1, f32[128,128]{1,0:T(8,128)} %energies.1, f32[128,128]{1,0:T(8,128)} %deviation.1, s32[2,192]{1,0:T(2,128)} %bitcast.11, s32[9,192]{1,0:T(8,128)} %bitcast.10, s32[1,192]{1,0:T(1,128)} %bitcast.12), custom_call_target="tpu_custom_call" | custom-call | tf_op jit(solution)/shard_map/rates/pallas_call | solution.py:362
  142.5 0.0 copy-done.1
  142.5 0.0 copy-done
  142.5 1.3 fusion
Async XLA Ops:
  0.6 141.9 %copy-start.1 = (f32[8,128]{1,0:T(8,128)S(1)}, f32[8,128]{1,0:T(8,128)}, u32[]{:S(2)}) copy-start(f32[8,128]{1,0:T(8,128)} %param.16) | copy-start | bytes 12292
  0.6 141.9 %copy-start = (f32[8,128]{1,0:T(8,128)S(1)}, f32[8,128]{1,0:T(8,128)}, u32[]{:S(2)}) copy-start(f32[8,128]{1,0:T(8,128)} %param.15) | copy-start | bytes 12292

commit v4 on v3

--- a/solution.py
+++ b/solution.py
@@ -13,6 +13,8 @@
 TILE = 16
 HALVES = 2
 ROUND = 2
+SINGLE = 4
+LAG = 3
 FIRST, SECOND, PLACE, START, SHIFT, MODE = range(6)
 
 MOVES = (
@@ -37,8 +39,8 @@
     blocks, rows, trans = coeffs.shape
     modes, trans_all = table.shape
     pair_total = block_pairs.shape[1]
-    rounds = other.shape[1]
-    pair_count = rounds * ROUND
+    pair_count = other.shape[1]
+    paired = HALVES * pair_count - SINGLE
     my_pb = lax.axis_index("pb")
     my_ta = lax.axis_index("ta")
     ta_count = part_in.shape[1]
@@ -127,20 +129,28 @@
             )
             copy.wait_recv()
 
-        def deliver(g, carry):
+        def deliver(s, count):
             for k, peer in enumerate(peers):
-                for u in range(ROUND):
-                    stage[h, g, k, u] = pieces[h][ints[FIRST, peer * pair_count + ROUND * g + u]]
+                for u in range(count):
+                    stage[h, s + u, k] = pieces[h][ints[FIRST, peer * pair_count + s + u]]
                 remote(
-                    stage.at[h, g, k],
-                    other.at[h, g, my_pb],
-                    send2.at[h, g], recv2.at[h, g], (peer, my_ta),
+                    stage.at[h, pl.ds(s, count), k], other.at[h, pl.ds(s, count), my_pb],
+                    send2.at[h, s], recv2.at[h, s], (peer, my_ta),
                 ).start()
-            for u in range(ROUND):
-                other[h, g, my_pb, u] = pieces[h][number(ROUND * g + u, FIRST)]
+            for u in range(count):
+                other[h, s + u, my_pb] = pieces[h][number(s + u, FIRST)]
+
+        def deliver_round(g, carry):
+            deliver(ROUND * g, ROUND)
             return carry
 
-        lax.fori_loop(0, rounds, deliver, 0)
+        def deliver_one(s, carry):
+            deliver(s, 1)
+            return carry
+
+        singles = SINGLE if h == HALVES - 1 else 0
+        lax.fori_loop(0, (pair_count - singles) // ROUND, deliver_round, 0)
+        lax.fori_loop(pair_count - singles, pair_count, deliver_one, 0)
 
     hand_on(0)
 
@@ -223,51 +233,57 @@
 
     pad = part_out.shape[2] - modes * strip
 
-    def flows_of(n):
-        for u in range(ROUND):
-            flows(n // rounds, ROUND * (n % rounds) + u)
+    def arrival(n, act):
+        h, s = n // pair_count, n % pair_count
+
+        def of(count):
+            part = other.at[h, pl.ds(s, count), pl.ds(0, n_peers)]
+            return remote(part, part, send2.at[h, s], recv2.at[h, s], (peers[0], my_ta))
+
+        @pl.when((n < paired) & (n % ROUND == 0))
+        def _():
+            act(of(ROUND))
+
+        @pl.when(n >= paired)
+        def _():
+            act(of(1))
 
     def couple(n, carry):
-        h, g = n // rounds, n % rounds
-
-        @pl.when(n > 1)
+        h, s = n // pair_count, n % pair_count
+
+        @pl.when(n >= LAG)
         def _():
-            flows_of(n - 2)
-
-        copy = remote(
-            stage.at[h, g], stage.at[h, g], send2.at[h, g], recv2.at[h, g], (peers[0], my_ta),
-        )
-        copy.wait_recv()
-        for u in range(ROUND):
-            s = ROUND * g + u
-            index = h * pair_count + s
-            for m in range(modes):
-                row = window[s, pl.ds(number(s, MODE + m), 1), :]
-                scale = jnp.broadcast_to(row, (TILE, trans)).astype(jnp.bfloat16)
-                for t in range(tiles):
-                    block = other[h, g, t, u].reshape(half // TILE, TILE, LANES)
-                    block = block * scale[None, :, t * LANES:(t + 1) * LANES]
-                    scaled[m * half:(m + 1) * half, t * LANES:(t + 1) * LANES] = block.reshape(half, LANES)
-            product = lax.dot_general(
-                scaled[...], held[number(s, PLACE)],
-                (((1,), (1,)), ((), ())), preferred_element_type=jnp.float32,
-            ).reshape(modes, ta_count, strip, rows)
-            for q in range(ta_count):
-                part = jnp.concatenate(
-                    [product[:, q].reshape(modes * strip, rows), jnp.zeros((pad, rows), jnp.float32)], axis=0
-                )
-                part_out[index, q] = part.astype(jnp.bfloat16)
-            for mate in mates:
-                remote(
-                    part_out.at[index, mate], part_in.at[index, my_ta],
-                    send3.at[index], recv3.at[index], (my_pb, mate),
-                ).start()
-            part_in[index, my_ta] = part_out[index, my_ta]
+            flows((n - LAG) // pair_count, (n - LAG) % pair_count)
+
+        arrival(n, lambda copy: copy.wait_recv())
+        index = n
+        for m in range(modes):
+            row = window[s, pl.ds(number(s, MODE + m), 1), :]
+            scale = jnp.broadcast_to(row, (TILE, trans)).astype(jnp.bfloat16)
+            for t in range(tiles):
+                block = other[h, s, t].reshape(half // TILE, TILE, LANES)
+                block = block * scale[None, :, t * LANES:(t + 1) * LANES]
+                scaled[m * half:(m + 1) * half, t * LANES:(t + 1) * LANES] = block.reshape(half, LANES)
+        product = lax.dot_general(
+            scaled[...], held[number(s, PLACE)],
+            (((1,), (1,)), ((), ())), preferred_element_type=jnp.float32,
+        ).reshape(modes, ta_count, strip, rows)
+        for q in range(ta_count):
+            part = jnp.concatenate(
+                [product[:, q].reshape(modes * strip, rows), jnp.zeros((pad, rows), jnp.float32)], axis=0
+            )
+            part_out[index, q] = part.astype(jnp.bfloat16)
+        for mate in mates:
+            remote(
+                part_out.at[index, mate], part_in.at[index, my_ta],
+                send3.at[index], recv3.at[index], (my_pb, mate),
+            ).start()
+        part_in[index, my_ta] = part_out[index, my_ta]
         return carry
 
-    lax.fori_loop(0, HALVES * rounds, couple, 0)
-    for n in range(HALVES * rounds - 2, HALVES * rounds):
-        flows_of(n)
+    lax.fori_loop(0, HALVES * pair_count, couple, 0)
+    for s in range(pair_count - LAG, pair_count):
+        flows(HALVES - 1, s)
 
     used = 2 * HALVES * strip
     stacked = jnp.concatenate(
@@ -294,17 +310,12 @@
             ).wait_send()
 
     def sent(n, carry):
-        h, g = n // rounds, n % rounds
-        remote(
-            stage.at[h, g], stage.at[h, g], send2.at[h, g], recv2.at[h, g], (peers[0], my_ta),
-        ).wait_send()
-        for u in range(ROUND):
-            index = ROUND * n + u
-            block = part_in.at[index, pl.ds(0, n_mates)]
-            remote(block, block, send3.at[index], recv3.at[index], (my_pb, mates[0])).wait_send()
+        arrival(n, lambda copy: copy.wait_send())
+        block = part_in.at[n, pl.ds(0, n_mates)]
+        remote(block, block, send3.at[n], recv3.at[n], (my_pb, mates[0])).wait_send()
         return carry
 
-    lax.fori_loop(0, HALVES * rounds, sent, 0)
+    lax.fori_loop(0, HALVES * pair_count, sent, 0)
 
     few = first_in.at[pl.ds(0, n_peers)]
     sums = remote(few, few, send4.at[0], recv4.at[0], (peers[0], my_ta))
@@ -351,7 +362,6 @@
     ta_count = lax.axis_size("ta")
     half = rows // HALVES
     strip = half // ta_count
-    rounds = PAIRS_DEV // ROUND
     units = HALVES * PAIRS_DEV
     padded = -(-modes * strip // TILE) * TILE
     list_lanes = -(-pair_total // LANES) * LANES
@@ -361,15 +371,15 @@
     dma = pltpu.SemaphoreType.DMA
     flow = pl.pallas_call(
         kernel,
-        out_shape=jax.ShapeDtypeStruct((2, blocks, rows), f32),
+        out_shape=pltpu.VMEM((2, blocks, rows), f32),
         in_specs=[smem, pl.BlockSpec(memory_space=pl.ANY)] + [vmem] * 6,
         out_specs=vmem,
         scratch_shapes=[
             pltpu.VMEM((blocks, rows, trans), bf16),
             pltpu.VMEM((pb_count * blocks, half, LANES), bf16),
             pltpu.VMEM((pb_count * blocks, half, LANES), bf16),
-            pltpu.VMEM((HALVES, rounds, pb_count - 1, ROUND, half, LANES), bf16),
-            pltpu.VMEM((HALVES, rounds, pb_count, ROUND, half, LANES), bf16),
+            pltpu.VMEM((HALVES, PAIRS_DEV, pb_count - 1, half, LANES), bf16),
+            pltpu.VMEM((HALVES, PAIRS_DEV, pb_count, half, LANES), bf16),
             pltpu.VMEM((modes * half, trans), bf16),
             pltpu.VMEM((units, ta_count, padded, rows), bf16),
             pltpu.VMEM((units, ta_count, padded, rows), bf16),
@@ -390,7 +400,7 @@
             pltpu.VMEM((ta_count, blocks, LANES), f32),
             dma((2,)),
             dma((HALVES, pb_count - 1)), dma((HALVES, pb_count - 1)),
-            dma((HALVES, rounds)), dma((HALVES, rounds)),
+            dma((HALVES, PAIRS_DEV)), dma((HALVES, PAIRS_DEV)),
             dma((units,)), dma((units,)),
             dma((3,)), dma((3,)),
         ],

time: 144 us -> 141 us (0.979)
  Pallas kernels: 142 us -> 140 us
    pallas_call x1, Pallas kernels: 142 us -> 140 us  [shards(): pl.pallas_call(kernel, out_shape=pltpu.VMEM((2, blocks, rows), f32), in_s...]
where the time goes in v4:
time: 141 us
  Pallas kernels  140 us (99%)
    pallas_call x1, Pallas kernels, shards(): pl.pallas_call(kernel, out_shape=pltpu.VMEM((2, blocks, rows), f32), in_s...  140 us

profile of v4, /device:TPU:1, one launch (start us, length us, event | category | flops | bytes accessed | tf_op | source)
XLA Modules:
  0.0 140.9 jit_solution(6994627133259695471)
XLA Ops:
  0.6 0.0 copy-start.1
  0.6 0.0 copy-start
  0.7 139.7 %rates.1 = f32[2,8,128]{2,1,0:T(8,128)S(1)} custom-call(f32[9]{0:T(128)} %phonon.1, bf16[8,128,2048]{2,1,0:T(8,128)(2,1)} %coeffs.1, bf16[9,16384]{1,0:T(8,128)(2,1)} %table.1, f32[128,128]{1,0:T(8,128)} %energies.1, f32[128,128]{1,0:T(8,128)} %deviation.1, s32[2,192]{1,0:T(2,128)} %bitcast.11, s32[9,192]{1,0:T(8,128)} %bitcast.10, s32[1,192]{1,0:T(1,128)} %bitcast.12), custom_call_target="tpu_custom_call" | custom-call | tf_op jit(solution)/shard_map/rates/pallas_call | solution.py:372
  140.3 0.0 copy-done.1
  140.3 0.0 copy-done
  140.3 0.6 fusion
Async XLA Ops:
  0.6 139.7 %copy-start.1 = (f32[8,128]{1,0:T(8,128)S(1)}, f32[8,128]{1,0:T(8,128)}, u32[]{:S(2)}) copy-start(f32[8,128]{1,0:T(8,128)} %param.16) | copy-start | bytes 12292
  0.6 139.7 %copy-start = (f32[8,128]{1,0:T(8,128)S(1)}, f32[8,128]{1,0:T(8,128)}, u32[]{:S(2)}) copy-start(f32[8,128]{1,0:T(8,128)} %param.15) | copy-start | bytes 12292

commit v5 on v4

--- a/solution.py
+++ b/solution.py
@@ -14,12 +14,19 @@
 HALVES = 2
 ROUND = 2
 SINGLE = 4
-LAG = 3
-FIRST, SECOND, PLACE, START, SHIFT, MODE = range(6)
-
-MOVES = (
-    (1, 0), (0, 1), (2, 2), (3, 0), (0, 3), (2, 1), (1, 1), (1, 2),
-    (3, 3), (2, 3), (1, 3), (3, 2), (3, 1), (2, 0), (0, 2),
+LAG = 4
+FIRST, SECOND, PLACE, START, SHIFT, SWAPPED, MODE = range(7)
+
+SIDE = 4
+KINDS = 2
+COPIES = 2
+SPREAD = (
+    (1, 0, 0), (0, 1, 0), (3, 0, 1), (0, 3, 0), (1, 1, 0), (0, 2, 0), (3, 3, 1),
+    (0, 1, 1), (1, 3, 0), (0, 3, 1), (3, 1, 1), (1, 2, 0), (0, 2, 1), (3, 2, 1),
+)
+GIVE = (
+    (1, 0, 1), (0, 1, 0), (3, 0, 0), (0, 3, 0), (1, 1, 1), (0, 2, 0), (3, 3, 0),
+    (0, 1, 1), (1, 3, 1), (0, 3, 1), (3, 1, 0), (1, 2, 1), (0, 2, 1), (3, 2, 0),
 )
 FAR_MOVES = (
     (2, 2), (2, 1), (1, 2), (2, 3), (3, 2), (1, 1), (3, 3), (1, 3),
@@ -34,27 +41,28 @@
     held, pieces_a, pieces_b, stage, other, scaled, part_out, part_in,
     weight_f, weight_b, value_a, wide, window, turn, lists, ints,
     acc_first, acc_second, first_out, first_in, second_in, total, total_in,
-    local, send1, recv1, send2, recv2, send3, recv3, send4, recv4,
+    local, send1, recv1, send2, recv2, send3, recv3, send4, recv4, send5, recv5,
 ):
     blocks, rows, trans = coeffs.shape
     modes, trans_all = table.shape
     pair_total = block_pairs.shape[1]
-    pair_count = other.shape[1]
+    pair_count = other.shape[2]
     paired = HALVES * pair_count - SINGLE
     my_pb = lax.axis_index("pb")
     my_ta = lax.axis_index("ta")
     ta_count = part_in.shape[1]
     half = rows // HALVES
     strip = half // ta_count
-    my_y, my_z = my_pb // 4, my_pb % 4
-    peers = [((my_y + dy) % 4) * 4 + (my_z + dz) % 4 for dy, dz in MOVES]
+    my_y, my_z = my_pb // SIDE, my_pb % SIDE
+    places = (my_y, my_z)
+    share = half // KINDS
     far_peers = [((my_y + dy) % 4) * 4 + (my_z + dz) % 4 for dy, dz in FAR_MOVES]
     mates = [(my_ta + d) % ta_count for d in MATES]
-    n_peers, n_mates = len(peers), len(mates)
+    n_peers, n_mates = len(far_peers), len(mates)
     pieces = (pieces_a, pieces_b)
 
     barrier = pltpu.get_barrier_semaphore()
-    for peer in peers:
+    for peer in far_peers:
         pl.semaphore_signal(barrier, inc=1, device_id=(peer, my_ta), device_id_type=MESH)
     for mate in mates:
         pl.semaphore_signal(barrier, inc=1, device_id=(my_pb, mate), device_id_type=MESH)
@@ -68,19 +76,34 @@
             device_id=device, device_id_type=MESH,
         )
 
-    my_lane = pl.multiple_of(my_pb * LANES, LANES)
+    def coords(t):
+        return places[t], places[1 - t]
+
+    def device(t, main, side):
+        return main * SIDE + side if t == 0 else side * SIDE + main
+
+    def lane_of(t, main, side):
+        return pl.ds(pl.multiple_of(device(t, main, side) * LANES, LANES), LANES)
+
+    def blocks_of(main, side):
+        return pl.ds((main * SIDE + side) * blocks, blocks)
+
+    def rows_of(h, t):
+        return pl.ds(h * half + t * share, share)
+
+    def back(place, copy):
+        return (place + SIDE - copy) % SIDE
+
     for h in range(HALVES):
-        def spread(g, carry, h=h):
-            for k, peer in enumerate(peers):
-                lane = pl.multiple_of(peer * LANES, LANES)
+        for first, second, copy in SPREAD:
+            for t in range(KINDS):
+                main, side = coords(t)
+                to_main, to_side = (main + first) % SIDE, (side + second) % SIDE
                 remote(
-                    coeffs.at[pl.ds(ROUND * g, ROUND), pl.ds(h * half, half), pl.ds(lane, LANES)],
-                    pieces[h].at[pl.ds(my_pb * blocks + ROUND * g, ROUND)],
-                    send1.at[h, k], recv1.at[h, k], (peer, my_ta),
+                    coeffs.at[:, rows_of(h, t), lane_of(t, back(to_main, copy), to_side)],
+                    pieces[h].at[t, copy, blocks_of(main, side)],
+                    send1.at[h, t], recv1.at[h, t], (device(t, to_main, to_side), my_ta),
                 ).start()
-            return carry
-
-        lax.fori_loop(0, blocks // ROUND, spread, 0)
 
     shift_of = blocks.bit_length() - 1
     spread_lanes = lists.shape[1]
@@ -103,9 +126,16 @@
     hot = lax.broadcasted_iota(jnp.int32, (pair_total, spread_lanes), 1) == slot
     start = column_form[:, 2:3] + my_ta * trans
     start = jnp.where(start >= trans_all, start - trans_all, start)
+
+    def swap(block):
+        owner_of = lax.shift_right_logical(block, shift_of)
+        swapped = (owner_of & (SIDE - 1)) * SIDE + lax.shift_right_logical(owner_of, SIDE.bit_length() - 1)
+        return swapped * blocks + (block & (blocks - 1))
+
     columns = [
         column_form[:, 0:1], second, second & (blocks - 1),
         lax.shift_right_logical(start, 7), start & (LANES - 1),
+        swap(column_form[:, 0:1]),
     ] + [column_form[:, MODE + m:MODE + m + 1] for m in range(modes)]
     for c, column in enumerate(columns):
         lists[c:c + 1, :] = jnp.sum(jnp.where(hot, column, 0), axis=0, keepdims=True)
@@ -114,31 +144,60 @@
     fetch.wait()
     listing.wait()
     for h in range(HALVES):
-        pieces[h][pl.ds(my_pb * blocks, blocks)] = held[:, pl.ds(h * half, half), pl.ds(my_lane, LANES)]
+        for t in range(KINDS):
+            main, side = coords(t)
+            for copy in range(COPIES):
+                pieces[h][t, copy, blocks_of(main, side)] = held[:, rows_of(h, t), lane_of(t, back(main, copy), side)]
 
     def number(s, which):
         return ints[which, my_pb * pair_count + s]
 
+    def spread_of(h, t):
+        part = stage.at[h, t, pl.ds(0, blocks)]
+        return remote(part, part, send1.at[h, t], recv1.at[h, t], (far_peers[0], my_ta))
+
+    def copies_of(h, t):
+        part = pieces[h].at[t, 0]
+        return remote(part, part, send5.at[h, t], recv5.at[h, t], (far_peers[0], my_ta))
+
     def hand_on(h):
-        for k, peer in enumerate(peers):
-            lane = pl.multiple_of(peer * LANES, LANES)
-            copy = remote(
-                coeffs.at[:, pl.ds(h * half, half), pl.ds(lane, LANES)],
-                pieces[h].at[pl.ds(my_pb * blocks, blocks)],
-                send1.at[h, k], recv1.at[h, k], (peer, my_ta),
-            )
-            copy.wait_recv()
+        for t in range(KINDS):
+            spread_of(h, t).wait_recv()
+        for w in range(SIDE):
+            for t in range(KINDS):
+                main, side = coords(t)
+                for copy, move in ((0, 1), (1, SIDE - 1)):
+                    to = (main + move) % SIDE
+                    for origin in (main, (main + SIDE - move) % SIDE):
+                        remote(
+                            pieces[h].at[t, copy, blocks_of(origin, w)], pieces[h].at[t, 1 - copy, blocks_of(origin, w)],
+                            send5.at[h, t], recv5.at[h, t], (device(t, to, side), my_ta),
+                        ).start()
+
+    def give_out(h):
+        for t in range(KINDS):
+            copies_of(h, t).wait_recv()
+
+        def piece(t, copy, place, s):
+            return pieces[h][t, copy, ints[SWAPPED if t else FIRST, place * pair_count + s]]
 
         def deliver(s, count):
-            for k, peer in enumerate(peers):
-                for u in range(count):
-                    stage[h, s + u, k] = pieces[h][ints[FIRST, peer * pair_count + s + u]]
-                remote(
-                    stage.at[h, pl.ds(s, count), k], other.at[h, pl.ds(s, count), my_pb],
-                    send2.at[h, s], recv2.at[h, s], (peer, my_ta),
-                ).start()
-            for u in range(count):
-                other[h, s + u, my_pb] = pieces[h][number(s + u, FIRST)]
+            for k, (first, second, copy) in enumerate(GIVE):
+                for t in range(KINDS):
+                    main, side = coords(t)
+                    to = device(t, (main + first) % SIDE, (side + second) % SIDE)
+                    for u in range(count):
+                        stage[h, t, s + u, k] = piece(t, copy, to, s + u)
+                    remote(
+                        stage.at[h, t, pl.ds(s, count), k],
+                        other.at[h, t, pl.ds(s, count), device(t, back(main, copy), side)],
+                        send2.at[h, t, s], recv2.at[h, t, s], (to, my_ta),
+                    ).start()
+            for t in range(KINDS):
+                main, side = coords(t)
+                for copy in range(COPIES):
+                    for u in range(count):
+                        other[h, t, s + u, device(t, back(main, copy), side)] = piece(t, copy, my_pb, s + u)
 
         def deliver_round(g, carry):
             deliver(ROUND * g, ROUND)
@@ -152,7 +211,9 @@
         lax.fori_loop(0, (pair_count - singles) // ROUND, deliver_round, 0)
         lax.fori_loop(pair_count - singles, pair_count, deliver_one, 0)
 
-    hand_on(0)
+    for h in range(HALVES):
+        hand_on(h)
+    give_out(0)
 
     wide[...] = jnp.zeros_like(wide)
     tiles_all = trans_all // LANES
@@ -203,7 +264,7 @@
 
     lax.fori_loop(0, pair_count, prepare, 0)
     for h in range(1, HALVES):
-        hand_on(h)
+        give_out(h)
 
     def flows(h, s):
         index = h * pair_count + s
@@ -236,17 +297,19 @@
     def arrival(n, act):
         h, s = n // pair_count, n % pair_count
 
-        def of(count):
-            part = other.at[h, pl.ds(s, count), pl.ds(0, n_peers)]
-            return remote(part, part, send2.at[h, s], recv2.at[h, s], (peers[0], my_ta))
+        def of(t, count):
+            part = stage.at[h, t, pl.ds(s, count)]
+            return remote(part, part, send2.at[h, t, s], recv2.at[h, t, s], (far_peers[0], my_ta))
 
         @pl.when((n < paired) & (n % ROUND == 0))
         def _():
-            act(of(ROUND))
+            for t in range(KINDS):
+                act(of(t, ROUND))
 
         @pl.when(n >= paired)
         def _():
-            act(of(1))
+            for t in range(KINDS):
+                act(of(t, 1))
 
     def couple(n, carry):
         h, s = n // pair_count, n % pair_count
@@ -261,9 +324,11 @@
             row = window[s, pl.ds(number(s, MODE + m), 1), :]
             scale = jnp.broadcast_to(row, (TILE, trans)).astype(jnp.bfloat16)
             for t in range(tiles):
-                block = other[h, s, t].reshape(half // TILE, TILE, LANES)
-                block = block * scale[None, :, t * LANES:(t + 1) * LANES]
-                scaled[m * half:(m + 1) * half, t * LANES:(t + 1) * LANES] = block.reshape(half, LANES)
+                for kind in range(KINDS):
+                    block = other[h, kind, s, t].reshape(share // TILE, TILE, LANES)
+                    block = block * scale[None, :, t * LANES:(t + 1) * LANES]
+                    low = m * half + kind * share
+                    scaled[low:low + share, t * LANES:(t + 1) * LANES] = block.reshape(share, LANES)
         product = lax.dot_general(
             scaled[...], held[number(s, PLACE)],
             (((1,), (1,)), ((), ())), preferred_element_type=jnp.float32,
@@ -301,13 +366,9 @@
     second_in[my_ta] = acc_second[...]
 
     for h in range(HALVES):
-        for k, peer in enumerate(peers):
-            lane = pl.multiple_of(peer * LANES, LANES)
-            remote(
-                coeffs.at[:, pl.ds(h * half, half), pl.ds(lane, LANES)],
-                pieces[h].at[pl.ds(my_pb * blocks, blocks)],
-                send1.at[h, k], recv1.at[h, k], (peer, my_ta),
-            ).wait_send()
+        for t in range(KINDS):
+            spread_of(h, t).wait_send()
+            copies_of(h, t).wait_send()
 
     def sent(n, carry):
         arrival(n, lambda copy: copy.wait_send())
@@ -318,7 +379,7 @@
     lax.fori_loop(0, HALVES * pair_count, sent, 0)
 
     few = first_in.at[pl.ds(0, n_peers)]
-    sums = remote(few, few, send4.at[0], recv4.at[0], (peers[0], my_ta))
+    sums = remote(few, few, send4.at[0], recv4.at[0], (far_peers[0], my_ta))
     sums.wait_recv()
     total[...] = jnp.sum(first_in[...], axis=0)
     for mate in mates:
@@ -361,6 +422,7 @@
     pb_count = lax.axis_size("pb")
     ta_count = lax.axis_size("ta")
     half = rows // HALVES
+    share = half // KINDS
     strip = half // ta_count
     units = HALVES * PAIRS_DEV
     padded = -(-modes * strip // TILE) * TILE
@@ -376,10 +438,10 @@
         out_specs=vmem,
         scratch_shapes=[
             pltpu.VMEM((blocks, rows, trans), bf16),
-            pltpu.VMEM((pb_count * blocks, half, LANES), bf16),
-            pltpu.VMEM((pb_count * blocks, half, LANES), bf16),
-            pltpu.VMEM((HALVES, PAIRS_DEV, pb_count - 1, half, LANES), bf16),
-            pltpu.VMEM((HALVES, PAIRS_DEV, pb_count, half, LANES), bf16),
+            pltpu.VMEM((KINDS, COPIES, pb_count * blocks, share, LANES), bf16),
+            pltpu.VMEM((KINDS, COPIES, pb_count * blocks, share, LANES), bf16),
+            pltpu.VMEM((HALVES, KINDS, PAIRS_DEV, len(GIVE), share, LANES), bf16),
+            pltpu.VMEM((HALVES, KINDS, PAIRS_DEV, pb_count, share, LANES), bf16),
             pltpu.VMEM((modes * half, trans), bf16),
             pltpu.VMEM((units, ta_count, padded, rows), bf16),
             pltpu.VMEM((units, ta_count, padded, rows), bf16),
@@ -399,10 +461,11 @@
             pltpu.VMEM((blocks, LANES), f32),
             pltpu.VMEM((ta_count, blocks, LANES), f32),
             dma((2,)),
-            dma((HALVES, pb_count - 1)), dma((HALVES, pb_count - 1)),
-            dma((HALVES, PAIRS_DEV)), dma((HALVES, PAIRS_DEV)),
+            dma((HALVES, KINDS)), dma((HALVES, KINDS)),
+            dma((HALVES, KINDS, PAIRS_DEV)), dma((HALVES, KINDS, PAIRS_DEV)),
             dma((units,)), dma((units,)),
             dma((3,)), dma((3,)),
+            dma((HALVES, KINDS)), dma((HALVES, KINDS)),
         ],
         compiler_params=pltpu.CompilerParams(
             collective_id=0, has_side_effects=True, vmem_limit_bytes=56 << 20

time: 141 us -> 137 us (0.972)
  Pallas kernels: 140 us -> 135 us
    pallas_call x1, Pallas kernels: 140 us -> 135 us  [shards(): pl.pallas_call(kernel, out_shape=pltpu.VMEM((2, blocks, rows), f32), in_s...]
where the time goes in v5:
time: 137 us
  Pallas kernels  135 us (99%)
    pallas_call x1, Pallas kernels, shards(): pl.pallas_call(kernel, out_shape=pltpu.VMEM((2, blocks, rows), f32), in_s...  135 us

profile of v5, /device:TPU:1, one launch (start us, length us, event | category | flops | bytes accessed | tf_op | source)
XLA Modules:
  0.0 136.6 jit_solution(7128426464257528606)
XLA Ops:
  0.6 0.0 copy-start.1
  0.6 0.0 copy-start
  0.7 135.3 %rates.1 = f32[2,8,128]{2,1,0:T(8,128)S(1)} custom-call(f32[9]{0:T(128)} %phonon.1, bf16[8,128,2048]{2,1,0:T(8,128)(2,1)} %coeffs.1, bf16[9,16384]{1,0:T(8,128)(2,1)} %table.1, f32[128,128]{1,0:T(8,128)} %energies.1, f32[128,128]{1,0:T(8,128)} %deviation.1, s32[2,192]{1,0:T(2,128)} %bitcast.11, s32[9,192]{1,0:T(8,128)} %bitcast.10, s32[1,192]{1,0:T(1,128)} %bitcast.12), custom_call_target="tpu_custom_call" | custom-call | tf_op jit(solution)/shard_map/rates/pallas_call | solution.py:434
  136.0 0.0 copy-done.1
  136.0 0.0 copy-done
  136.0 0.6 fusion
Async XLA Ops:
  0.6 135.3 %copy-start.1 = (f32[8,128]{1,0:T(8,128)S(1)}, f32[8,128]{1,0:T(8,128)}, u32[]{:S(2)}) copy-start(f32[8,128]{1,0:T(8,128)} %param.16) | copy-start | bytes 12292
  0.6 135.3 %copy-start = (f32[8,128]{1,0:T(8,128)S(1)}, f32[8,128]{1,0:T(8,128)}, u32[]{:S(2)}) copy-start(f32[8,128]{1,0:T(8,128)} %param.15) | copy-start | bytes 12292

commit v6 on v5

--- a/solution.py
+++ b/solution.py
@@ -13,11 +13,12 @@
 TILE = 16
 HALVES = 2
 ROUND = 2
-SINGLE = 4
+SINGLE = 8
 LAG = 4
 FIRST, SECOND, PLACE, START, SHIFT, SWAPPED, MODE = range(7)
 
 SIDE = 4
+BATCH = 4
 KINDS = 2
 COPIES = 2
 SPREAD = (
@@ -94,14 +95,14 @@
     def back(place, copy):
         return (place + SIDE - copy) % SIDE
 
-    for h in range(HALVES):
+    for h, part in [(h, part) for h in range(HALVES) for part in range(0, blocks, BATCH)]:
         for first, second, copy in SPREAD:
             for t in range(KINDS):
                 main, side = coords(t)
                 to_main, to_side = (main + first) % SIDE, (side + second) % SIDE
                 remote(
-                    coeffs.at[:, rows_of(h, t), lane_of(t, back(to_main, copy), to_side)],
-                    pieces[h].at[t, copy, blocks_of(main, side)],
+                    coeffs.at[pl.ds(part, BATCH), rows_of(h, t), lane_of(t, back(to_main, copy), to_side)],
+                    pieces[h].at[t, copy, pl.ds((main * SIDE + side) * blocks + part, BATCH)],
                     send1.at[h, t], recv1.at[h, t], (device(t, to_main, to_side), my_ta),
                 ).start()
 

time: 137 us -> 136 us (level)
  no operation moved by 1% of the time
where the time goes in v6:
time: 136 us
  Pallas kernels  134 us (99%)
    pallas_call x1, Pallas kernels, shards(): pl.pallas_call(kernel, out_shape=pltpu.VMEM((2, blocks, rows), f32), in_s...  134 us

profile of v6, /device:TPU:1, one launch (start us, length us, event | category | flops | bytes accessed | tf_op | source)
XLA Modules:
  0.0 135.6 jit_solution(1649885323277519418)
XLA Ops:
  0.6 0.0 copy-start.1
  0.6 0.0 copy-start
  0.7 134.3 %rates.1 = f32[2,8,128]{2,1,0:T(8,128)S(1)} custom-call(f32[9]{0:T(128)} %phonon.1, bf16[8,128,2048]{2,1,0:T(8,128)(2,1)} %coeffs.1, bf16[9,16384]{1,0:T(8,128)(2,1)} %table.1, f32[128,128]{1,0:T(8,128)} %energies.1, f32[128,128]{1,0:T(8,128)} %deviation.1, s32[2,192]{1,0:T(2,128)} %bitcast.11, s32[9,192]{1,0:T(8,128)} %bitcast.10, s32[1,192]{1,0:T(1,128)} %bitcast.12), custom_call_target="tpu_custom_call" | custom-call | tf_op jit(solution)/shard_map/rates/pallas_call | solution.py:435
  135.0 0.0 copy-done.1
  135.0 0.0 copy-done
  135.0 0.6 fusion
Async XLA Ops:
  0.6 134.4 %copy-start.1 = (f32[8,128]{1,0:T(8,128)S(1)}, f32[8,128]{1,0:T(8,128)}, u32[]{:S(2)}) copy-start(f32[8,128]{1,0:T(8,128)} %param.16) | copy-start | bytes 12292
  0.6 134.4 %copy-start = (f32[8,128]{1,0:T(8,128)S(1)}, f32[8,128]{1,0:T(8,128)}, u32[]{:S(2)}) copy-start(f32[8,128]{1,0:T(8,128)} %param.15) | copy-start | bytes 12292

commit v7 on v6

--- a/solution.py
+++ b/solution.py
@@ -26,8 +26,8 @@
     (0, 1, 1), (1, 3, 0), (0, 3, 1), (3, 1, 1), (1, 2, 0), (0, 2, 1), (3, 2, 1),
 )
 GIVE = (
-    (1, 0, 1), (0, 1, 0), (3, 0, 0), (0, 3, 0), (1, 1, 1), (0, 2, 0), (3, 3, 0),
-    (0, 1, 1), (1, 3, 1), (0, 3, 1), (3, 1, 0), (1, 2, 1), (0, 2, 1), (3, 2, 0),
+    (1, 0, 1), (0, 1, 0), (3, 2, 0), (0, 3, 1), (1, 1, 1), (3, 0, 0), (0, 2, 0),
+    (1, 3, 1), (0, 1, 1), (3, 3, 0), (0, 3, 0), (1, 2, 1), (3, 1, 0), (0, 2, 1),
 )
 FAR_MOVES = (
     (2, 2), (2, 1), (1, 2), (2, 3), (3, 2), (1, 1), (3, 3), (1, 3),
@@ -377,7 +377,7 @@
         remote(block, block, send3.at[n], recv3.at[n], (my_pb, mates[0])).wait_send()
         return carry
 
-    lax.fori_loop(0, HALVES * pair_count, sent, 0)
+    lax.fori_loop(0, pair_count, sent, 0)
 
     few = first_in.at[pl.ds(0, n_peers)]
     sums = remote(few, few, send4.at[0], recv4.at[0], (far_peers[0], my_ta))
@@ -386,6 +386,7 @@
     for mate in mates:
         remote(total, total_in.at[my_ta], send4.at[2], recv4.at[2], (my_pb, mate)).start()
     total_in[my_ta] = total[...]
+    lax.fori_loop(pair_count, HALVES * pair_count, sent, 0)
     sums.wait_send()
     for ref, sem in ((second_in, 1), (total_in, 2)):
         few = ref.at[pl.ds(0, n_mates)]

time: 136 us -> 135 us (level)
  no operation moved by 1% of the time
where the time goes in v7:
time: 135 us
  Pallas kernels  134 us (99%)
    pallas_call x1, Pallas kernels, shards(): pl.pallas_call(kernel, out_shape=pltpu.VMEM((2, blocks, rows), f32), in_s...  134 us

profile of v7, /device:TPU:1, one launch (start us, length us, event | category | flops | bytes accessed | tf_op | source)
XLA Modules:
  0.0 135.1 jit_solution(9755434353868602788)
XLA Ops:
  0.6 0.0 copy-start.1
  0.6 0.0 copy-start
  0.7 133.8 %rates.1 = f32[2,8,128]{2,1,0:T(8,128)S(1)} custom-call(f32[9]{0:T(128)} %phonon.1, bf16[8,128,2048]{2,1,0:T(8,128)(2,1)} %coeffs.1, bf16[9,16384]{1,0:T(8,128)(2,1)} %table.1, f32[128,128]{1,0:T(8,128)} %energies.1, f32[128,128]{1,0:T(8,128)} %deviation.1, s32[2,192]{1,0:T(2,128)} %bitcast.11, s32[9,192]{1,0:T(8,128)} %bitcast.10, s32[1,192]{1,0:T(1,128)} %bitcast.12), custom_call_target="tpu_custom_call" | custom-call | tf_op jit(solution)/shard_map/rates/pallas_call | solution.py:436
  134.4 0.0 copy-done.1
  134.4 0.0 copy-done
  134.5 0.6 fusion
Async XLA Ops:
  0.6 133.8 %copy-start.1 = (f32[8,128]{1,0:T(8,128)S(1)}, f32[8,128]{1,0:T(8,128)}, u32[]{:S(2)}) copy-start(f32[8,128]{1,0:T(8,128)} %param.16) | copy-start | bytes 12292
  0.6 133.8 %copy-start = (f32[8,128]{1,0:T(8,128)S(1)}, f32[8,128]{1,0:T(8,128)}, u32[]{:S(2)}) copy-start(f32[8,128]{1,0:T(8,128)} %param.15) | copy-start | bytes 12292

commit v8 on v7

--- a/solution.py
+++ b/solution.py
@@ -22,8 +22,8 @@
 KINDS = 2
 COPIES = 2
 SPREAD = (
-    (1, 0, 0), (0, 1, 0), (3, 0, 1), (0, 3, 0), (1, 1, 0), (0, 2, 0), (3, 3, 1),
-    (0, 1, 1), (1, 3, 0), (0, 3, 1), (3, 1, 1), (1, 2, 0), (0, 2, 1), (3, 2, 1),
+    (1, 0, 0), (0, 1, 0), (3, 2, 1), (0, 3, 1), (1, 1, 0), (3, 0, 1), (0, 2, 0),
+    (1, 3, 0), (0, 1, 1), (3, 3, 1), (0, 3, 0), (1, 2, 0), (3, 1, 1), (0, 2, 1),
 )
 GIVE = (
     (1, 0, 1), (0, 1, 0), (3, 2, 0), (0, 3, 1), (1, 1, 1), (3, 0, 0), (0, 2, 0),

time: 135 us -> 135 us (level)
  no operation moved by 1% of the time
where the time goes in v8:
time: 135 us
  Pallas kernels  134 us (99%)
    pallas_call x1, Pallas kernels, shards(): pl.pallas_call(kernel, out_shape=pltpu.VMEM((2, blocks, rows), f32), in_s...  134 us

profile of v8, /device:TPU:1, one launch (start us, length us, event | category | flops | bytes accessed | tf_op | source)
XLA Modules:
  0.0 135.1 jit_solution(8194578905512608161)
XLA Ops:
  0.6 0.0 copy-start.1
  0.6 0.0 copy-start
  0.7 133.8 %rates.1 = f32[2,8,128]{2,1,0:T(8,128)S(1)} custom-call(f32[9]{0:T(128)} %phonon.1, bf16[8,128,2048]{2,1,0:T(8,128)(2,1)} %coeffs.1, bf16[9,16384]{1,0:T(8,128)(2,1)} %table.1, f32[128,128]{1,0:T(8,128)} %energies.1, f32[128,128]{1,0:T(8,128)} %deviation.1, s32[2,192]{1,0:T(2,128)} %bitcast.11, s32[9,192]{1,0:T(8,128)} %bitcast.10, s32[1,192]{1,0:T(1,128)} %bitcast.12), custom_call_target="tpu_custom_call" | custom-call | tf_op jit(solution)/shard_map/rates/pallas_call | solution.py:436
  134.4 0.0 copy-done.1
  134.4 0.0 copy-done
  134.5 0.6 fusion
Async XLA Ops:
  0.6 133.8 %copy-start.1 = (f32[8,128]{1,0:T(8,128)S(1)}, f32[8,128]{1,0:T(8,128)}, u32[]{:S(2)}) copy-start(f32[8,128]{1,0:T(8,128)} %param.16) | copy-start | bytes 12292
  0.6 133.8 %copy-start = (f32[8,128]{1,0:T(8,128)S(1)}, f32[8,128]{1,0:T(8,128)}, u32[]{:S(2)}) copy-start(f32[8,128]{1,0:T(8,128)} %param.15) | copy-start | bytes 12292
